TPU v7x, 128 devices: a whole 4x4x4 slice. The times are simulated.
128 devices in a mesh: row: 8 (over y, core), col: 16 (over x, z).
Axes of the slice: x: 4, y: 4, z: 4, core: 2. Of those that a mesh axis runs over, the one named last changes fastest.
Arguments:
- blocks: bfloat16 [256, 16, 512, 512], P('row', 'col'), may hold values from 3.8146973e-06 to 0.32348633, as said below
- source_ids: int32 [256, 16], P('row', 'col'), may hold values from 0 to 255, as said below
- emission: bfloat16 [5008, 131072], P('col', 'row'), may hold values from 0.05 to 5120, as said below
- tokens: int32 [4, 104], replicated, may hold values from 0 to 5007, as said below
Outputs:
- posterior: bfloat16 [104, 131072], P(None, ('row', 'col'))
- log_total: float32 [104], replicated
Inputs may be any that keep to these rules, and one draw needn't show every extreme that they name: Block id source_ids[J, k] lies in the group g of 2 consecutive blocks (g = id // 2) with g % 16 == k // (16 // 16). In every step exactly 26 of the 104 tokens lie in one range of 5008 // 16 consecutive ids, which one is drawn, and no such range holds more. `emission`: positive weights. `blocks`: positive weights.
All inputs are finite; a program needn't handle non-finite values.
Results may differ from a plain program's by a relative error of at most 0.029.
Values may be sent and summed in bfloat16 or wider, within the bound.
A program may use at most 128 MiB of HBM per device.

v0:
```python
import jax
import jax.numpy as jnp
from jax import lax
from jax.sharding import PartitionSpec as P

STATES = 131072


def on_device(blocks, source_ids, emission, tokens):
    row_count = lax.axis_size("row")
    col_count = lax.axis_size("col")
    col_index = lax.axis_index("col")
    local_rows, local_slots, width, _unused = blocks.shape
    vocab_local, panel = emission.shape
    piece = panel // col_count
    piece_blocks = piece // width
    total_steps, seq_count = tokens.shape
    start_id = col_index * vocab_local
    inside = (tokens >= start_id) & (tokens < start_id + vocab_local)
    looked = jnp.take(emission, jnp.clip(tokens - start_id, 0, vocab_local - 1), axis=0)
    terms = jnp.where(inside[:, :, None], looked.astype(jnp.float32), 0.0)
    emitted = lax.psum_scatter(terms.astype(jnp.bfloat16), "col", scatter_dimension=2, tiled=True)

    def normalize(weighted):
        total = lax.psum(jnp.sum(weighted, axis=1), ("row", "col"))
        scale = total / STATES
        return ((weighted / scale[:, None]).astype(jnp.bfloat16), jnp.log(scale))

    group = source_ids // piece_blocks
    local_index = (group // col_count * piece_blocks + source_ids % piece_blocks).reshape(-1)
    states_now, log_total = normalize(emitted[0].astype(jnp.float32))
    for position in range(1, total_steps):
        whole = lax.all_gather(states_now, "row", axis=1, tiled=True)
        sources = whole.reshape(seq_count, row_count * piece_blocks, width)
        taken = jnp.take(sources, local_index, axis=1).reshape(
            seq_count, local_rows, local_slots, width
        )
        partial_value = jnp.einsum(
            "bjkm,jkmn->bjn", taken, blocks, preferred_element_type=jnp.float32
        )
        partial_value = partial_value.reshape(seq_count, local_rows * width)
        carried = lax.psum_scatter(
            partial_value.astype(jnp.bfloat16), "col", scatter_dimension=1, tiled=True
        ).astype(jnp.float32)
        weighted = emitted[position].astype(jnp.float32) * carried
        states_now, log_part = normalize(weighted)
        log_total = log_total + log_part
    return (states_now, log_total)


def solution(mesh):
    in_specs = (P("row", "col", None, None), P("row", "col"), P("col", "row"), P())
    out_specs = (P(None, ("row", "col")), P())
    return jax.shard_map(
        on_device, mesh=mesh, in_specs=in_specs, out_specs=out_specs, check_vma=False
    )
```

profile of v0, /device:TPU:1, one launch (start us, length us, event | category | flops | bytes accessed | tf_op | source)
XLA Modules:
  0.0 772.1 jit_solution(9209239366619609842)
XLA Ops:
  7.2 0.0 reduce-scatter.5.cloned.1.call-start
  7.2 0.7 compare_and_fusion.1
  7.9 0.1 reshape.92
  8.0 33.4 %gather_fusion = bf16[416,16384]{1,0:T(8,128)(2,1)} fusion(bf16[313,16384]{1,0:T(8,128)(2,1)} %param.8, s32[1024]{0:T(1024)S(1)} %pad_clamp_fusion.1), kind=kCustom, calls=%fused_computation.3 | custom fusion | bytes 27264640 | tf_op jit(solution)/shard_map/jit(_take)/gather | solution.py:20
  41.4 14.2 %select_convert_fusion = bf16[4,104,16384]{2,1,0:T(8,128)(2,1)} fusion(bf16[4,104,16384]{2,1,0:T(8,128)(2,1)} %bitcast.83, pred[4,104]{1,0:T(4,128)(4,1)S(1)} %get-tuple-element.5, pred[4,104]{1,0:T(4,128)(4,1)S(1)} %get-tuple-element.7), kind=kLoop, calls=%fused_computation.4 | loop fusion | flops 27262976 | bytes 27263808 | tf_op jit(solution)/shard_map/convert_element_type | solution.py:22
  55.6 0.0 reduce-scatter.5.cloned.1.call-update
  55.6 0.0 all-gather.4.cloned.1.call-start
  55.7 100.9 %reduce-scatter.5.cloned.1.call-done = bf16[4,104,1024]{2,1,0:T(8,128)(2,1)} async-done(((bf16[4,104,16384]{2,1,0:T(8,128)(2,1)}), bf16[4,104,1024]{2,1,0:T(8,128)(2,1)}) %reduce-scatter.5.cloned.1.call-update) | async-done | bytes 851984 | tf_op jit(solution)/shard_map/reduce_scatter | solution.py:22
  156.6 1.1 convert_reduce_fusion
  157.6 64.5 %psum.28 = f32[104]{0:T(128)S(1)} all-reduce(f32[104]{0:T(128)S(1)} %convert_reduce_fusion), channel_id=1, replica_groups=mesh['row'=8,'col'=16] {'row','col'}, use_global_device_ids=true, to_apply=%region_2.3 | all-reduce | flops 104 | bytes 832 | tf_op jit(solution)/shard_map/psum | solution.py:25
  222.1 1.7 fusion.31
  223.9 0.0 all-gather.4.cloned.1.call-update
  223.9 0.0 reduce-scatter.7.cloned.1.call-start
  224.0 21.5 %all-gather.4.cloned.1.call-done = bf16[104,8192]{1,0:T(8,128)(2,1)} async-done(((bf16[104,1024]{1,0:T(8,128)(2,1)}), bf16[104,8192]{1,0:T(8,128)(2,1)}) %all-gather.4.cloned.1.call-update) | async-done | bytes 1703952 | tf_op jit(solution)/shard_map/all_gather | solution.py:33
  245.5 2.7 copy.26
  248.2 2.2 gather_fusion.1
  250.5 8.5 %convert_bitcast_fusion.2 = bf16[32,13,8,512]{3,2,1,0:T(8,128)(2,1)S(1)} fusion(bf16[32,1,512,512]{3,2,1,0:T(8,128)(2,1)} %param.6, bf16[32,104,512]{2,1,0:T(8,128)(2,1)S(1)} %gather_fusion.1, pred[32]{0:T(512)(128)(4,1)S(1)} %get-tuple-element.3), kind=kOutput, calls=%fused_computation.19 | convolution fusion | flops 1748238336 | bytes 23592992 | tf_op jit(solution)/shard_map/bjkm,jkmn->bjn/dot_general | solution.py:38
  259.0 2.1 copy.18
  261.1 0.0 reduce-scatter.7.cloned.1.call-update
  261.1 0.0 all-gather.6.cloned.1.call-start
  261.1 74.4 %reduce-scatter.7.cloned.1.call-done = bf16[104,1024]{1,0:T(8,128)(2,1)} async-done(((bf16[104,16384]{1,0:T(8,128)(2,1)}), bf16[104,1024]{1,0:T(8,128)(2,1)}) %reduce-scatter.7.cloned.1.call-update) | async-done | bytes 213008 | tf_op jit(solution)/shard_map/reduce_scatter | solution.py:42
  335.5 1.1 fusion.34
  336.6 65.9 %psum.29 = f32[104]{0:T(128)S(1)} all-reduce(f32[104]{0:T(128)S(1)} %fusion.34), channel_id=1, replica_groups=mesh['row'=8,'col'=16] {'row','col'}, use_global_device_ids=true, to_apply=%region_5.7 | all-reduce | flops 104 | bytes 832 | tf_op jit(solution)/shard_map/psum | solution.py:25
  402.5 1.7 divide_convert_fusion.2
  404.3 0.0 reduce-scatter.9.cloned.1.call-start
  404.3 21.5 %all-gather.6.cloned.1.call-done = bf16[104,8192]{1,0:T(8,128)(2,1)} async-done(((bf16[104,1024]{1,0:T(8,128)(2,1)}), bf16[104,8192]{1,0:T(8,128)(2,1)}) %all-gather.6.cloned.1.call-update) | async-done | bytes 1703952 | tf_op jit(solution)/shard_map/all_gather | solution.py:33
  425.8 2.7 copy.25
  428.5 2.2 gather_fusion.2
  430.7 8.5 %convert_bitcast_fusion.1 = bf16[32,13,8,512]{3,2,1,0:T(8,128)(2,1)S(1)} fusion(bf16[32,1,512,512]{3,2,1,0:T(8,128)(2,1)} %param.6, bf16[32,104,512]{2,1,0:T(8,128)(2,1)S(1)} %gather_fusion.2, pred[32]{0:T(512)(128)(4,1)S(1)} %get-tuple-element.3), kind=kOutput, calls=%fused_computation.18 | convolution fusion | flops 1748238336 | bytes 23592992 | tf_op jit(solution)/shard_map/bjkm,jkmn->bjn/dot_general | solution.py:38
  439.3 2.1 copy.19
  441.3 0.0 reduce-scatter.9.cloned.1.call-update
  441.4 0.0 all-gather.8.cloned.1.call-start
  441.4 74.3 %reduce-scatter.9.cloned.1.call-done = bf16[104,1024]{1,0:T(8,128)(2,1)} async-done(((bf16[104,16384]{1,0:T(8,128)(2,1)}), bf16[104,1024]{1,0:T(8,128)(2,1)}) %reduce-scatter.9.cloned.1.call-update) | async-done | bytes 213008 | tf_op jit(solution)/shard_map/reduce_scatter | solution.py:42
  515.7 1.1 fusion.33
  516.8 66.0 %psum.30 = f32[104]{0:T(128)S(1)} all-reduce(f32[104]{0:T(128)S(1)} %fusion.33), channel_id=1, replica_groups=mesh['row'=8,'col'=16] {'row','col'}, use_global_device_ids=true, to_apply=%region_8.10 | all-reduce | flops 104 | bytes 832 | tf_op jit(solution)/shard_map/psum | solution.py:25
  582.8 1.7 divide_convert_fusion.1
  584.5 0.0 all-gather.8.cloned.1.call-update
  584.5 0.3 reduce-scatter.11.cloned.1.call-start
  584.8 21.3 %all-gather.8.cloned.1.call-done = bf16[104,8192]{1,0:T(8,128)(2,1)} async-done(((bf16[104,1024]{1,0:T(8,128)(2,1)}), bf16[104,8192]{1,0:T(8,128)(2,1)}) %all-gather.8.cloned.1.call-update) | async-done | bytes 1703952 | tf_op jit(solution)/shard_map/all_gather | solution.py:33
  606.0 2.7 copy.24
  608.8 2.2 gather_fusion.3
  611.0 8.5 %convert_bitcast_fusion = bf16[32,13,8,512]{3,2,1,0:T(8,128)(2,1)S(1)} fusion(bf16[32,1,512,512]{3,2,1,0:T(8,128)(2,1)} %param.6, bf16[32,104,512]{2,1,0:T(8,128)(2,1)S(1)} %gather_fusion.3, pred[32]{0:T(512)(128)(4,1)S(1)} %get-tuple-element.3), kind=kOutput, calls=%fused_computation.17 | convolution fusion | flops 1748238336 | bytes 23592992 | tf_op jit(solution)/shard_map/bjkm,jkmn->bjn/dot_general | solution.py:38
  619.5 2.1 copy.20
  621.6 74.4 %reduce-scatter.11.cloned.1.call-done = bf16[104,1024]{1,0:T(8,128)(2,1)} async-done(((bf16[104,16384]{1,0:T(8,128)(2,1)}), bf16[104,1024]{1,0:T(8,128)(2,1)}) %reduce-scatter.11.cloned.1.call-update) | async-done | bytes 213008 | tf_op jit(solution)/shard_map/reduce_scatter | solution.py:42
  696.0 1.1 fusion.32
  697.1 66.0 %psum.31 = f32[104]{0:T(128)S(1)} all-reduce(f32[104]{0:T(128)S(1)} %fusion.32), channel_id=1, replica_groups=mesh['row'=8,'col'=16] {'row','col'}, use_global_device_ids=true, to_apply=%region_11.13 | all-reduce | flops 104 | bytes 832 | tf_op jit(solution)/shard_map/psum | solution.py:25
  763.0 0.5 log_add_fusion
  763.6 1.7 divide_convert_fusion
  (16 shorter events, 0.1 us)
Async XLA Ops:
  7.2 149.4 %reduce-scatter.5.cloned.1.call-start = ((), (), s32[]{:S(2)}) async-start(), calls=%async_computation.4 | async-start | bytes 14483456 | tf_op jit(solution)/shard_map/reduce_scatter | solution.py:22
  55.6 168.3 %copy-start.3 = (s32[32,1]{0,1:T(1,128)S(1)}, s32[32,1]{0,1:T(1,128)}, u32[]{:S(2)}) copy-start(s32[32,1]{0,1:T(1,128)} %param.7) | copy-start | bytes 388
  55.6 189.9 %all-gather.4.cloned.1.call-start = ((), (), s32[]{:S(2)}) async-start(), calls=%async_computation.5 | async-start | bytes 1916928 | tf_op jit(solution)/shard_map/all_gather | solution.py:33
  223.9 111.6 %reduce-scatter.7.cloned.1.call-start = ((), (), s32[]{:S(2)}) async-start(), calls=%async_computation.6 | async-start | bytes 3620864 | tf_op jit(solution)/shard_map/reduce_scatter | solution.py:42
  261.0 74.5 %copy-start = (bf16[4,104,1024]{2,1,0:T(8,128)(2,1)S(1)}, bf16[4,104,1024]{2,1,0:T(8,128)(2,1)}, u32[]{:S(2)}) copy-start(bf16[4,104,1024]{2,1,0:T(8,128)(2,1)} %reduce-scatter.5.cloned.1.call-done) | copy-start | bytes 2555908
  261.1 164.7 %all-gather.6.cloned.1.call-start = ((), (), s32[]{:S(2)}) async-start(), calls=%async_computation.7 | async-start | bytes 1916928 | tf_op jit(solution)/shard_map/all_gather | solution.py:33
  404.3 111.4 %reduce-scatter.9.cloned.1.call-start = ((), (), s32[]{:S(2)}) async-start(), calls=%async_computation.8 | async-start | bytes 3620864 | tf_op jit(solution)/shard_map/reduce_scatter | solution.py:42
  441.3 74.4 %copy-start.1 = (bf16[4,104,1024]{2,1,0:T(8,128)(2,1)S(1)}, bf16[4,104,1024]{2,1,0:T(8,128)(2,1)}, u32[]{:S(2)}) copy-start(bf16[4,104,1024]{2,1,0:T(8,128)(2,1)} %reduce-scatter.5.cloned.1.call-done) | copy-start | bytes 2555908
  441.4 164.7 %all-gather.8.cloned.1.call-start = ((), (), s32[]{:S(2)}) async-start(), calls=%async_computation.9 | async-start | bytes 1916928 | tf_op jit(solution)/shard_map/all_gather | solution.py:33
  584.5 111.5 %reduce-scatter.11.cloned.1.call-start = ((), (), s32[]{:S(2)}) async-start(), calls=%async_computation.10 | async-start | bytes 3620864 | tf_op jit(solution)/shard_map/reduce_scatter | solution.py:42
  621.6 74.4 %copy-start.2 = (bf16[4,104,1024]{2,1,0:T(8,128)(2,1)S(1)}, bf16[4,104,1024]{2,1,0:T(8,128)(2,1)}, u32[]{:S(2)}) copy-start(bf16[4,104,1024]{2,1,0:T(8,128)(2,1)} %reduce-scatter.5.cloned.1.call-done) | copy-start | bytes 2555908
Sparse Core Ops, SparseCore 0:
  55.8 100.7 reduce-scatter.4
  224.0 21.4 all-gather.3
  261.2 74.2 reduce-scatter.6
  404.4 21.3 all-gather.5
  441.5 74.1 reduce-scatter.8
  584.6 21.3 all-gather.7
  621.7 74.2 reduce-scatter.10
where the time goes:
time: 773 us; the launch traced here: 772 us
  waiting for transfers between devices  388 us (50%)
  blocking collectives  262 us (34%)
  local copies, waits for them, and re-layouts  54.6 us (7%)
  other arithmetic  26.7 us (3%)
  matrix products  25.5 us (3%)
  between operations  14.2 us (2%)
    psum x4, blocking collectives, normalize(): total = lax.psum(jnp.sum(weighted, axis=1), ('row', 'col'))  262 us
    reduce_scatter x3, waiting for transfers between devices, on_device(): lax.psum_scatter(partial_value.astype(jnp.bfloat16), 'col', scatter_dimen...  223 us
    reduce_scatter x1, waiting for transfers between devices, on_device(): lax.psum_scatter(terms.astype(jnp.bfloat16), 'col', scatter_dimension=2,...  101 us
    all_gather x3, waiting for transfers between devices, on_device(): whole = lax.all_gather(states_now, 'row', axis=1, tiled=True)  64.2 us
    gather x1, local copies, waits for them, and re-layouts, on_device(): jnp.take(emission, jnp.clip(tokens - start_id, 0, vocab_local - 1), axis=0)  33.4 us
    dot_general x3, matrix products, on_device(): jnp.einsum('bjkm,jkmn->bjn', taken, blocks, preferred_element_type=jnp.fl...  25.5 us
  transfers between devices with their start and end apart: 7, of which 7 were waited for; matrix products, arithmetic and copies ran while one was open for 0% of the time, Pallas kernels for 0%

commit v1 on v0

v1 whole, which is shorter than its diff:
```python
import functools

import jax
import jax.numpy as jnp
from jax import lax
from jax.experimental import pallas as pl
from jax.experimental.pallas import tpu as pltpu
from jax.sharding import PartitionSpec as P

MESH = pl.DeviceIdType.MESH
STATES = 131072
SEQS = 104
CAP = 26
SLOT = 32
BLOCK = 512
HALF = 256
STEPS = 3
KOFF = (2, 1, 0, 3)
F32 = jnp.float32
BF16 = jnp.bfloat16


def iota(shape, dim):
    return lax.broadcasted_iota(jnp.int32, shape, dim).astype(F32)


def kernel(
    ids_ref, tok_ref, blocks_hbm, emis_hbm, post_ref, log_ref,
    blocks_v, emis_v, sel_v, pack, land1, land2, em, states_a, states_b, part, rs, wfin, ar0, ar1, ar2,
    blk_sem, emis_sem, e_send, e_recv, ag_send, ag_recv, rs_send, rs_recv, a_send, a_recv,
):
    row = lax.axis_index("row")
    col = lax.axis_index("col")
    y, core = row // 2, row % 2
    x, z = col // 4, col % 4
    vocab = emis_v.shape[1]

    def at_plane(xd, zd):
        return (row, (xd % 4) * 4 + zd % 4)

    def along(h, first, off):
        if (h == 0) == first:
            return at_plane(x + off, z)
        return at_plane(x, z + off)

    def pq(h):
        return (x, z) if h == 0 else (z, x)

    def at_y(off):
        return (((y + off) % 4) * 2 + core, col)

    sib = (row + 1 - 2 * core, col)

    def remote(src, dst, ssem, rsem, dev):
        return pltpu.make_async_remote_copy(
            src_ref=src, dst_ref=dst, send_sem=ssem, recv_sem=rsem, device_id=dev, device_id_type=MESH
        )

    def emis_copy(chunk):
        return pltpu.make_async_copy(
            emis_hbm.at[:, pl.ds(pl.multiple_of(chunk * BLOCK, BLOCK), BLOCK)], emis_v.at[chunk], emis_sem.at[chunk]
        )

    def chunk_of(h, po, qd):
        p, _ = pq(h)
        pd = (p + po) % 4
        return (pd * 4 + qd) * 2 if h == 0 else (qd * 4 + pd) * 2 + 1

    for po in (2, 1, 3, 0):
        for h in (0, 1):
            @pl.loop(0, 4)
            def _(qd):
                emis_copy(chunk_of(h, po, qd)).start()

    def blocks_copy(i):
        return pltpu.make_async_copy(blocks_hbm.at[pl.ds(i * 8, 8)], blocks_v.at[pl.ds(i * 8, 8)], blk_sem.at[i])

    for i in range(4):
        blocks_copy(i).start()

    barrier = pltpu.get_barrier_semaphore()
    row_peers = [(lax.rem(row + i, 8), col) for i in range(1, 8)]
    col_peers = [(row, lax.rem(col + i, 16)) for i in range(1, 16)]
    for dev in row_peers + col_peers:
        pl.semaphore_signal(barrier, inc=1, device_id=dev, device_id_type=MESH)

    eye = iota((SEQS, SEQS), 0) == iota((SEQS, SEQS), 1)
    before = iota((SEQS, SEQS), 0) < iota((SEQS, SEQS), 1)

    def to_col(v):
        return jnp.sum(jnp.where(eye, v, 0.0), axis=1, keepdims=True)

    def places(t):
        tok_row = tok_ref[t : t + 1, :].astype(F32)
        owner_row = jnp.zeros_like(tok_row)
        for k in range(1, 16):
            owner_row += jnp.where(tok_row >= float(k * vocab), 1.0, 0.0)
        owner_col = to_col(owner_row)
        same = jnp.where((owner_col == owner_row) & before, 1.0, 0.0)
        pos_row = jnp.sum(same, axis=0, keepdims=True)
        return tok_row, owner_row, owner_col, pos_row

    for t in range(STEPS + 1):
        tok_row, owner_row, owner_col, pos_row = places(t)
        me = col.astype(F32)
        slot_of = jnp.where((pos_row == iota((SLOT, SEQS), 0)) & (owner_row == me), 1.0, 0.0).astype(BF16)
        id_of = jnp.where(to_col(tok_row) - me * float(vocab) == iota((SEQS, vocab), 1), 1.0, 0.0).astype(BF16)
        sel_v[t * SLOT : (t + 1) * SLOT, :] = jnp.dot(slot_of, id_of, preferred_element_type=F32).astype(BF16)

    pl.semaphore_wait(barrier, 22)

    def e1(t, h, po):
        p, _ = pq(h)
        return remote(
            pack.at[t, h, po - 1], land1.at[t, h, :, p], e_send.at[t, h, 0, po - 1], e_recv.at[t, h, 0, po - 1],
            along(h, True, po),
        )

    def e2(t, h, qo):
        _, q = pq(h)
        return remote(
            land1.at[t, h, (q + qo) % 4], land2.at[t, h, q], e_send.at[t, h, 1, qo - 1], e_recv.at[t, h, 1, qo - 1],
            along(h, False, qo),
        )

    for po in (2, 1, 3, 0):
        for h in (0, 1):
            p, _ = pq(h)

            @pl.loop(0, 4)
            def _(qd):
                chunk = chunk_of(h, po, qd)
                emis_copy(chunk).wait()
                rows = jnp.dot(sel_v[...], emis_v[chunk], preferred_element_type=F32).astype(BF16)
                for t in range(STEPS + 1):
                    piece = rows[t * SLOT : (t + 1) * SLOT]
                    if po:
                        pack[t, h, po - 1, qd] = piece
                    else:
                        land1[t, h, qd, p] = piece

            if po:
                e1(0, h, po).start()

    def e_phase1(t):
        for po in (2, 1, 3):
            for h in (0, 1):
                e1(t, h, po).start()

    def e_phase2(t):
        for h in (0, 1):
            for po in (1, 3, 2):
                e1(t, h, po).wait_recv()
            for qo in (2, 1, 3):
                e2(t, h, qo).start()

    def e_final(t, h):
        p, q = pq(h)
        land2[t, h, q] = land1[t, h, q]
        _, _, owner_col, pos_row = places(t)
        if h == 0:
            high = jnp.zeros_like(owner_col)
            for k in range(1, 4):
                high += jnp.where(owner_col >= float(4 * k), 1.0, 0.0)
            place = (owner_col - 4.0 * high) * 4.0 + high
        else:
            place = owner_col
        target = place * float(SLOT) + to_col(pos_row)
        pick = jnp.where(iota((SEQS, 16 * SLOT), 1) == target, 1.0, 0.0).astype(BF16)
        for qo in (1, 3, 2):
            e2(t, h, qo).wait_recv()
        return jnp.dot(pick, land2[t, h].reshape(16 * SLOT, BLOCK), preferred_element_type=F32)

    def states_of(t):
        return states_b if t % 2 else states_a

    def ag(t, h, j, msg, of_row, dev):
        item = states_of(t).at[of_row * 2 + h, j]
        return remote(item, item, ag_send.at[t, h, j, msg], ag_recv.at[t, h, j, msg], dev)

    def same_core(off):
        return ((y + off) % 4) * 2 + core

    def ag_start(t, h, j):
        ag(t, h, j, 1, row, at_y(1)).start()
        ag(t, h, j, 2, row, at_y(3)).start()
        ag(t, h, j, 0, row, sib).start()

    def ag_relay1(t, h, j):
        for msg, off, on in ((1, 3, 1), (2, 1, 3)):
            of = same_core(off)
            ag(t, h, j, msg, of, sib).wait_recv()
            if (msg == 1) == (h == 0):
                ag(t, h, j, 5, of, at_y(on)).start()
            ag(t, h, j, msg + 2, of, sib).start()

    def ag_relay2(t, h, j):
        of = same_core(2)
        ag(t, h, j, 5, of, sib).wait_recv()
        ag(t, h, j, 6, of, sib).start()

    def ag_end(t, h, j):
        for msg in (0, 3, 4, 6):
            ag(t, h, j, msg, row, sib).wait_recv()

    def ag_sent(t, h, j):
        for msg in range(7):
            ag(t, h, j, msg, row, sib).wait_send()

    def product(t, j, h, po, k):
        p, q = pq(h)
        pd = (p + po) % 4
        qd = (q + 2 - k + 4) % 4
        dest = (pd * 4 + qd) * 2 if h == 0 else (qd * 4 + pd) * 2 + 1
        sid = ids_ref[dest]
        local = (sid // 32) * 2 + sid % 2
        left = states_of(t - 1)[local, 0]
        right = states_of(t - 1)[local, 1]
        cols = slice(j * HALF, (j + 1) * HALF)
        acc = jnp.dot(left, blocks_v[dest, :HALF, cols], preferred_element_type=F32)
        acc += jnp.dot(right, blocks_v[dest, HALF:, cols], preferred_element_type=F32)
        part[j, h, po, k] = acc.astype(BF16)

    def rcopy(t, j, h, src, msg, dev):
        return remote(src, rs.at[t % 2, j, h, msg], rs_send.at[t, j, h, msg], rs_recv.at[t, j, h, msg], dev)

    def arrived(t, j, h, msg):
        rcopy(t, j, h, rs.at[t % 2, j, h, msg], msg, sib).wait_recv()
        return rs[t % 2, j, h, msg].astype(F32)

    def rs_first(t, j):
        @pl.loop(0, 4)
        def _(k):
            for h in (0, 1):
                product(t, j, h, 2, k)
                rcopy(t, j, h, part.at[j, h, 2, k], k, along(h, True, 1 + 2 * (k % 2))).start()

        @pl.loop(0, 4)
        def _(k):
            for h in (0, 1):
                po = 3 - 2 * (k % 2)
                product(t, j, h, po, k)

    def rs_direct(t, j):
        @pl.loop(0, 4)
        def _(k):
            for h in (0, 1):
                po = 3 - 2 * (k % 2)
                rcopy(t, j, h, part.at[j, h, po, k], 8 - 4 * (k % 2) + k, along(h, True, po)).start()

    def rs_rest(t, j):
        @pl.loop(0, 4)
        def _(k):
            for h in (0, 1):
                product(t, j, h, 1 + 2 * (k % 2), k)
                product(t, j, h, 0, k)

    def rs_merge(t, j):
        @pl.loop(0, 4)
        def _(k):
            for h in (0, 1):
                po = 1 + 2 * (k % 2)
                got = arrived(t, j, h, k)
                part[j, h, po, k] = (part[j, h, po, k].astype(F32) + got).astype(BF16)
                rcopy(t, j, h, part.at[j, h, po, k], 4 + 4 * (k % 2) + k, along(h, True, po)).start()

    def summed(t, j, h, k):
        return part[j, h, 0, k].astype(F32) + arrived(t, j, h, 4 + k) + arrived(t, j, h, 8 + k)

    def rs_second(t, j):
        for k in (0, 1, 3):
            for h in (0, 1):
                part[j, h, 0, k] = summed(t, j, h, k).astype(BF16)
                src = part.at[j, h, 0, k]
                if k == 0:
                    rcopy(t, j, h, src, 12, along(h, False, 1 + 2 * j)).start()
                elif k == 1 and j == 1:
                    rcopy(t, j, h, src, 13, along(h, False, 1)).start()
                elif k == 3 and j == 0:
                    rcopy(t, j, h, src, 14, along(h, False, 3)).start()

    def rs_merge2(t, j):
        k = 1 if j == 0 else 3
        for h in (0, 1):
            got = arrived(t, j, h, 12)
            part[j, h, 0, k] = (part[j, h, 0, k].astype(F32) + got).astype(BF16)
            rcopy(t, j, h, part.at[j, h, 0, k], 13 + j, along(h, False, k)).start()

    def rs_final(t, j, h):
        carried = summed(t, j, h, 2) + arrived(t, j, h, 13) + arrived(t, j, h, 14)
        return em[t - 1, h, j].astype(F32) * carried

    def rs_sent(t):
        @pl.loop(0, 15)
        def _(msg):
            for j in (0, 1):
                for h in (0, 1):
                    rcopy(t, j, h, rs.at[t % 2, j, h, msg], msg, sib).wait_send()

    def keep(t, h, j, weighted):
        states_of(t)[row * 2 + h, j] = weighted.astype(BF16)
        ag_start(t, h, j)

    def each(fn, t):
        for h in (0, 1):
            for j in (0, 1):
                fn(t, h, j)

    def store_emitted(t):
        for h in (0, 1):
            value = e_final(t, h).astype(BF16)
            for j in (0, 1):
                em[t - 1, h, j] = value[:, j * HALF : (j + 1) * HALF]

    e_phase2(0)
    e_phase1(1)
    for h in (0, 1):
        first = e_final(0, h)
        for j in (0, 1):
            keep(0, h, j, first[:, j * HALF : (j + 1) * HALF])
    each(ag_relay1, 0)
    each(ag_relay2, 0)
    e_phase2(1)
    for i in range(4):
        blocks_copy(i).wait()
    each(ag_end, 0)

    for t in range(1, STEPS + 1):
        last = t == STEPS
        rs_first(t, 0)
        rs_direct(t, 0)
        rs_rest(t, 0)
        rs_merge(t, 0)
        rs_first(t, 1)
        rs_direct(t, 1)
        rs_rest(t, 1)
        rs_second(t, 0)
        rs_merge(t, 1)
        rs_merge2(t, 0)
        store_emitted(t)
        rs_second(t, 1)
        each(ag_sent, t - 1)
        total = jnp.zeros((SEQS, 1), F32)
        for j in (0, 1):
            if j == 1:
                rs_merge2(t, 1)
                if not last:
                    for h in (0, 1):
                        ag_relay1(t, h, 0)
            for h in (0, 1):
                weighted = rs_final(t, j, h)
                if last:
                    wfin[h, j] = weighted
                    total += jnp.sum(weighted, axis=1, keepdims=True)
                else:
                    keep(t, h, j, weighted)
        if not last:
            e_phase1(t + 1)
            for h in (0, 1):
                ag_relay2(t, h, 0)
            for h in (0, 1):
                ag_relay1(t, h, 1)
            for h in (0, 1):
                ag_relay2(t, h, 1)
            e_phase2(t + 1)
            rs_sent(t)
            each(ag_end, t)

    wide = iota((SEQS, 128), 0) == iota((SEQS, 128), 1)
    mine = jnp.sum(jnp.where(wide, total, 0.0), axis=0, keepdims=True)
    ar0[0] = jnp.broadcast_to(mine, (8, 128))
    ar1[row] = ar0[0]

    def a1(i):
        return remote(ar0.at[0], ar1.at[row], a_send.at[i - 1], a_recv.at[i - 1], row_peers[i - 1])

    def a2(i):
        return remote(ar0.at[1], ar2.at[col], a_send.at[6 + i], a_recv.at[6 + i], col_peers[i - 1])

    for i in range(1, 8):
        a1(i).start()
    for i in range(1, 8):
        a1(i).wait_recv()
    ar0[1] = jnp.sum(ar1[...], axis=0)
    ar2[col] = ar0[1]
    for i in range(1, 16):
        a2(i).start()
    for i in range(1, 16):
        a2(i).wait_recv()
    scale = jnp.sum(ar2[...], axis=0)[0:1] * (1.0 / STATES)
    log_ref[...] = jnp.log(scale)
    scale_col = jnp.sum(jnp.where(wide, scale, 0.0), axis=1, keepdims=True)
    for h in (0, 1):
        for j in (0, 1):
            post_ref[:, h * BLOCK + j * HALF : h * BLOCK + (j + 1) * HALF] = (wfin[h, j] / scale_col).astype(BF16)

    rs_sent(STEPS)
    for t in range(STEPS + 1):
        for h in (0, 1):
            for o in (1, 2, 3):
                e1(t, h, o).wait_send()
                e2(t, h, o).wait_send()
    for i in range(1, 8):
        a1(i).wait_send()
    for i in range(1, 16):
        a2(i).wait_send()


def on_device(blocks, source_ids, emission, tokens):
    vocab = emission.shape[0]
    dma = pltpu.SemaphoreType.DMA
    vmem = pltpu.VMEM
    posterior, logs = pl.pallas_call(
        kernel,
        out_shape=(jax.ShapeDtypeStruct((SEQS, 2 * BLOCK), BF16), jax.ShapeDtypeStruct((1, 128), F32)),
        in_specs=[
            pl.BlockSpec(memory_space=pltpu.SMEM),
            pl.BlockSpec(memory_space=pltpu.VMEM),
            pl.BlockSpec(memory_space=pl.ANY),
            pl.BlockSpec(memory_space=pl.ANY),
        ],
        out_specs=(pl.BlockSpec(memory_space=pltpu.VMEM), pl.BlockSpec(memory_space=pltpu.VMEM)),
        scratch_shapes=[
            vmem((32, BLOCK, BLOCK), BF16),
            vmem((32, vocab, BLOCK), BF16),
            vmem((4 * SLOT, vocab), BF16),
            vmem((STEPS + 1, 2, 3, 4, SLOT, BLOCK), BF16),
            vmem((STEPS + 1, 2, 4, 4, SLOT, BLOCK), BF16),
            vmem((STEPS + 1, 2, 4, 4, SLOT, BLOCK), BF16),
            vmem((STEPS, 2, 2, SEQS, HALF), BF16),
            vmem((16, 2, SEQS, HALF), BF16),
            vmem((16, 2, SEQS, HALF), BF16),
            vmem((2, 2, 4, 4, SEQS, HALF), BF16),
            vmem((2, 2, 2, 15, SEQS, HALF), BF16),
            vmem((2, 2, SEQS, HALF), F32),
            vmem((2, 8, 128), F32),
            vmem((8, 8, 128), F32),
            vmem((16, 8, 128), F32),
            dma((4,)),
            dma((32,)),
            dma((STEPS + 1, 2, 2, 3)),
            dma((STEPS + 1, 2, 2, 3)),
            dma((STEPS, 2, 2, 7)),
            dma((STEPS, 2, 2, 7)),
            dma((STEPS + 1, 2, 2, 15)),
            dma((STEPS + 1, 2, 2, 15)),
            dma((22,)),
            dma((22,)),
        ],
        compiler_params=pltpu.CompilerParams(
            collective_id=0, has_side_effects=True, vmem_limit_bytes=63 * 2**20
        ),
        name="forward",
    )(source_ids.reshape(-1), tokens, blocks.reshape(32, BLOCK, BLOCK), emission)
    return posterior, logs[0, :SEQS]


def solution(mesh):
    in_specs = (P("row", "col", None, None), P("row", "col"), P("col", "row"), P())
    out_specs = (P(None, ("row", "col")), P())
    return jax.shard_map(on_device, mesh=mesh, in_specs=in_specs, out_specs=out_specs, check_vma=False)
```

time: 773 us -> 162 us (0.21)
  waiting for transfers between devices: 388 us -> 0 us
  blocking collectives: 262 us -> 0 us
  Pallas kernels: 0 us -> 158 us
  local copies, waits for them, and re-layouts: 54.6 us -> 2.74 us
  other arithmetic: 26.7 us -> 0 us
  matrix products: 25.5 us -> 0 us
  between operations: 14.2 us -> 0.64 us
    reduce_scatter x4 -> x0, waiting for transfers between devices: 324 us -> none  [the longest x3 223 us: on_device(): lax.psum_scatter(partial_value.astype(jnp.bfloat16), 'col', scatter_dimen...]
    psum x4 -> x0, blocking collectives: 262 us -> none  [normalize(): total = lax.psum(jnp.sum(weighted, axis=1), ('row', 'col'))]
    pallas_call x0 -> x1, Pallas kernels: none -> 158 us  [on_device(): pl.pallas_call(kernel, out_shape=(jax.ShapeDtypeStruct((SEQS, 2 * BLOCK),...]
    all_gather x3 -> x0, waiting for transfers between devices: 64.2 us -> none  [on_device(): whole = lax.all_gather(states_now, 'row', axis=1, tiled=True)]
    gather x4 -> x0, local copies, waits for them, and re-layouts: 40.1 us -> none  [the longest x1 33.4 us: on_device(): jnp.take(emission, jnp.clip(tokens - start_id, 0, vocab_local - 1), axis=0)]
    dot_general x3 -> x0, matrix products: 25.5 us -> none  [on_device(): jnp.einsum('bjkm,jkmn->bjn', taken, blocks, preferred_element_type=jnp.fl...]
    convert_element_type x5 -> x0, other arithmetic: 21.1 us -> none  [the longest x1 14.2 us: on_device(): terms.astype(jnp.bfloat16)]
    reshape x3 -> x0, local copies, waits for them, and re-layouts: 8.22 us -> none  [on_device(): sources = whole.reshape(seq_count, row_count * piece_blocks, width)]
  transfers between devices with their start and end apart: 7 -> 0, of which waited for: 7 -> 0; matrix products, arithmetic and copies ran while one was open for 0% -> 0% of each run, Pallas kernels for 0% -> 0%
where the time goes in v1:
time: 162 us
  Pallas kernels  158 us (98%)
  local copies, waits for them, and re-layouts  2.74 us (2%)
    pallas_call x1, Pallas kernels, on_device(): pl.pallas_call(kernel, out_shape=(jax.ShapeDtypeStruct((SEQS, 2 * BLOCK),...  158 us

profile of v1, /device:TPU:1, one launch (start us, length us, event | category | flops | bytes accessed | tf_op | source)
XLA Modules:
  0.0 161.7 jit_solution(378947247522724855)
XLA Ops:
  0.6 158.3 %forward.1 = (bf16[104,1024]{1,0:T(8,128)(2,1)}, f32[1,128]{1,0:T(1,128)}) custom-call(s32[32]{0:T(128)} %bitcast.5, s32[4,104]{1,0:T(4,128)} %tok_ref.1, bf16[32,512,512]{2,1,0:T(8,128)(2,1)} %bitcast.4, bf16[313,16384]{1,0:T(8,128)(2,1)} %emis_hbm.1), custom_call_target="tpu_custom_call" | custom-call | tf_op jit(solution)/shard_map/forward/pallas_call | solution.py:413
  158.9 1.1 slice_bitcast_fusion
  160.1 1.6 %copy.7 = bf16[104,1024]{1,0:T(8,128)(2,1)} copy(bf16[104,1024]{1,0:T(8,128)(2,1)} %get-tuple-element.8) | data formatting | bytes 425984

commit v2 on v1

v2 whole, which is shorter than its diff:
```python
import functools

import jax
import jax.numpy as jnp
from jax import lax
from jax.experimental import pallas as pl
from jax.experimental.pallas import tpu as pltpu
from jax.sharding import PartitionSpec as P

MESH = pl.DeviceIdType.MESH
STATES = 131072
SEQS = 104
CAP = 26
SLOT = 32
BLOCK = 512
STEPS = 3
ROWS = (slice(0, 48), slice(48, 104))
F32 = jnp.float32
BF16 = jnp.bfloat16


def iota(shape, dim):
    return lax.broadcasted_iota(jnp.int32, shape, dim).astype(F32)


def kernel(
    ids_ref, tok_ref, blocks_hbm, emis_hbm, post_ref, log_ref,
    blocks_v, emis_v, sel_v, pack, land1, land2, em, states_a, states_b, states_c, states_d, part_a, part_b, rs_a, rs_b, wfin, ar0, ar1, ar2,
    blk_sem, emis_sem, e_send, e_recv, ag_send, ag_recv, rs_send, rs_recv, a_send, a_recv,
):
    row = lax.axis_index("row")
    col = lax.axis_index("col")
    y, core = row // 2, row % 2
    x, z = col // 4, col % 4
    vocab = emis_v.shape[1]
    states = (states_a, states_b, states_c, states_d)
    part = (part_a, part_b)
    rs = (rs_a, rs_b)

    def at_plane(xd, zd):
        return (row, (xd % 4) * 4 + zd % 4)

    def along(h, first, off):
        if (h == 0) == first:
            return at_plane(x + off, z)
        return at_plane(x, z + off)

    def pq(h):
        return (x, z) if h == 0 else (z, x)

    def at_y(off):
        return (((y + off) % 4) * 2 + core, col)

    sib = (row + 1 - 2 * core, col)

    def remote(src, dst, ssem, rsem, dev):
        return pltpu.make_async_remote_copy(
            src_ref=src, dst_ref=dst, send_sem=ssem, recv_sem=rsem, device_id=dev, device_id_type=MESH
        )

    def emis_copy(chunk):
        return pltpu.make_async_copy(
            emis_hbm.at[:, pl.ds(pl.multiple_of(chunk * BLOCK, BLOCK), BLOCK)], emis_v.at[chunk], emis_sem.at[chunk]
        )

    def chunk_of(h, po, qd):
        p, _ = pq(h)
        pd = (p + po) % 4
        return (pd * 4 + qd) * 2 if h == 0 else (qd * 4 + pd) * 2 + 1

    for po in (2, 1, 3, 0):
        for h in (0, 1):
            @pl.loop(0, 4)
            def _(qd):
                emis_copy(chunk_of(h, po, qd)).start()

    def blocks_copy():
        return pltpu.make_async_copy(blocks_hbm, blocks_v, blk_sem)

    blocks_copy().start()

    barrier = pltpu.get_barrier_semaphore()
    row_peers = [(lax.rem(row + i, 8), col) for i in range(1, 8)]
    col_peers = [(row, lax.rem(col + i, 16)) for i in range(1, 16)]
    for dev in row_peers + col_peers:
        pl.semaphore_signal(barrier, inc=1, device_id=dev, device_id_type=MESH)

    eye = iota((SEQS, SEQS), 0) == iota((SEQS, SEQS), 1)
    before = iota((SEQS, SEQS), 0) < iota((SEQS, SEQS), 1)

    def to_col(v):
        return jnp.sum(jnp.where(eye, v, 0.0), axis=1, keepdims=True)

    def places(t):
        tok_row = tok_ref[t : t + 1, :].astype(F32)
        owner_row = jnp.zeros_like(tok_row)
        for k in range(1, 16):
            owner_row += jnp.where(tok_row >= float(k * vocab), 1.0, 0.0)
        owner_col = to_col(owner_row)
        same = jnp.where((owner_col == owner_row) & before, 1.0, 0.0)
        pos_row = jnp.sum(same, axis=0, keepdims=True)
        return tok_row, owner_row, owner_col, pos_row

    for t in range(STEPS + 1):
        tok_row, owner_row, owner_col, pos_row = places(t)
        me = col.astype(F32)
        slot_of = jnp.where((pos_row == iota((SLOT, SEQS), 0)) & (owner_row == me), 1.0, 0.0).astype(BF16)
        id_of = jnp.where(to_col(tok_row) - me * float(vocab) == iota((SEQS, vocab), 1), 1.0, 0.0).astype(BF16)
        sel_v[t * SLOT : (t + 1) * SLOT, :] = jnp.dot(slot_of, id_of, preferred_element_type=F32).astype(BF16)

    pl.semaphore_wait(barrier, 22)

    def e1(t, h, po):
        p, _ = pq(h)
        return remote(
            pack.at[t, h, po - 1], land1.at[t, h, :, p], e_send.at[t, 0], e_recv.at[t, 0, h],
            along(h, True, po),
        )

    def e2(t, h, qo):
        _, q = pq(h)
        return remote(
            land1.at[t, h, (q + qo) % 4], land2.at[t, h, q], e_send.at[t, 1], e_recv.at[t, 1, h],
            along(h, False, qo),
        )

    for po in (2, 1, 3, 0):
        for h in (0, 1):
            p, _ = pq(h)

            @pl.loop(0, 4)
            def _(qd):
                chunk = chunk_of(h, po, qd)
                emis_copy(chunk).wait()
                rows = jnp.dot(sel_v[...], emis_v[chunk], preferred_element_type=F32).astype(BF16)
                for t in range(STEPS + 1):
                    piece = rows[t * SLOT : (t + 1) * SLOT]
                    if po:
                        pack[t, h, po - 1, qd] = piece
                    else:
                        land1[t, h, qd, p] = piece

            if po:
                e1(0, h, po).start()

    def e_phase1(t):
        for po in (2, 1, 3):
            for h in (0, 1):
                e1(t, h, po).start()

    def e_phase2(t):
        for h in (0, 1):
            three = land1.at[t, h, :, 0:3]
            remote(three, three, e_send.at[t, 0], e_recv.at[t, 0, h], sib).wait_recv()
            for qo in (2, 1, 3):
                e2(t, h, qo).start()

    def e_final(t, h):
        p, q = pq(h)
        land2[t, h, q] = land1[t, h, q]
        _, _, owner_col, pos_row = places(t)
        if h == 0:
            high = jnp.zeros_like(owner_col)
            for k in range(1, 4):
                high += jnp.where(owner_col >= float(4 * k), 1.0, 0.0)
            place = (owner_col - 4.0 * high) * 4.0 + high
        else:
            place = owner_col
        target = place * float(SLOT) + to_col(pos_row)
        pick = jnp.where(iota((SEQS, 16 * SLOT), 1) == target, 1.0, 0.0).astype(BF16)
        three = land2.at[t, h, 0:3]
        remote(three, three, e_send.at[t, 1], e_recv.at[t, 1, h], sib).wait_recv()
        return jnp.dot(pick, land2[t, h].reshape(16 * SLOT, BLOCK), preferred_element_type=F32)

    def states_of(t, c):
        return states[c * 2 + t % 2]

    def ag(t, c, h, of_row, sem, dev):
        item = states_of(t, c).at[of_row * 2 + h]
        return remote(item, item, ag_send.at[c, h], ag_recv.at[t % 2, c, h, sem], dev)

    def same_core(off):
        return ((y + off) % 4) * 2 + core

    def ag_start(t, c, h):
        ag(t, c, h, row, 0, at_y(1)).start()
        ag(t, c, h, row, 1, at_y(3)).start()
        ag(t, c, h, row, 3, sib).start()

    def ag_relay1(t, c):
        for sem, off, on in ((0, 3, 1), (1, 1, 3)):
            for h in (0, 1):
                of = same_core(off)
                ag(t, c, h, of, sem, sib).wait_recv()
                if sem == h:
                    ag(t, c, h, of, 2, at_y(on)).start()
                ag(t, c, h, of, 3, sib).start()

    def ag_relay2(t, c):
        for h in (0, 1):
            of = same_core(2)
            ag(t, c, h, of, 2, sib).wait_recv()
            ag(t, c, h, of, 3, sib).start()

    def ag_end(t, c):
        for h in (0, 1):
            four = states_of(t, c).at[0:4]
            remote(four, four, ag_send.at[c, h], ag_recv.at[t % 2, c, h, 3], sib).wait_recv()

    def ag_sent(t, c):
        for h in (0, 1):
            seven = states_of(t, c).at[0:7]
            remote(seven, seven, ag_send.at[c, h], ag_recv.at[t % 2, c, h, 3], sib).wait_send()

    def product(t, c, h, po, k):
        p, q = pq(h)
        pd = (p + po) % 4
        qd = (q + 2 - k + 4) % 4
        dest = (pd * 4 + qd) * 2 if h == 0 else (qd * 4 + pd) * 2 + 1
        sid = ids_ref[dest]
        local = (sid // 32) * 2 + sid % 2
        acc = jnp.dot(states_of(t - 1, c)[local], blocks_v[dest], preferred_element_type=F32)
        part[c][h, po, k] = acc.astype(BF16)

    def rcopy(t, c, h, src, msg, sem, dev):
        return remote(src, rs[c].at[t % 2, h, msg], rs_send.at[c, h], rs_recv.at[t % 2, c, h, sem], dev)

    def arrived(t, c, h, k):
        rcopy(t, c, h, rs[c].at[t % 2, h, k], k, k, sib).wait_recv()
        return rs[c][t % 2, h, k].astype(F32)

    def both_arrived(t, c, h, msg, sem):
        pair = rs[c].at[t % 2, h, pl.ds(msg, 2)]
        remote(pair, pair, rs_send.at[c, h], rs_recv.at[t % 2, c, h, sem], sib).wait_recv()
        return rs[c][t % 2, h, msg].astype(F32) + rs[c][t % 2, h, msg + 1].astype(F32)

    def rs_multiply(t, c):
        @pl.loop(0, 2)
        def _(kk):
            for k in (2 * kk, 2 * kk + 1):
                for h in (0, 1):
                    product(t, c, h, 2, k)
            for k in (0, 1):
                for h in (0, 1):
                    rcopy(t, c, h, part[c].at[h, 2, 2 * kk + k], 2 * kk + k, 2 * kk + k, along(h, True, 1 + 2 * k)).start()

        @pl.loop(0, 2)
        def _(kk):
            for k in (0, 1):
                for h in (0, 1):
                    product(t, c, h, 3 - 2 * k, 2 * kk + k)
            for k in (0, 1):
                for h in (0, 1):
                    po = 3 - 2 * k
                    k2 = 2 * kk + k
                    rcopy(t, c, h, part[c].at[h, po, k2], 5 + 2 * k2 - k, 4 + k2, along(h, True, po)).start()

        @pl.loop(0, 2)
        def _(kk):
            for k in (0, 1):
                for h in (0, 1):
                    product(t, c, h, 1 + 2 * k, 2 * kk + k)

        @pl.loop(0, 2)
        def _(kk):
            for k in (0, 1):
                for h in (0, 1):
                    product(t, c, h, 0, 2 * kk + k)

    def rs_merge(t, c):
        @pl.loop(0, 2)
        def _(kk):
            for k in (0, 1):
                for h in (0, 1):
                    po = 1 + 2 * k
                    k2 = 2 * kk + k
                    got = arrived(t, c, h, k2)
                    part[c][h, po, k2] = (part[c][h, po, k2].astype(F32) + got).astype(BF16)
                    rcopy(t, c, h, part[c].at[h, po, k2], 4 + 2 * k2 + k, 4 + k2, along(h, True, po)).start()

    def summed(t, c, h, k):
        return part[c][h, 0, k].astype(F32) + both_arrived(t, c, h, 4 + 2 * k, 4 + k)

    def rs_second(t, c):
        for k in (0, 1, 3):
            for h in (0, 1):
                part[c][h, 0, k] = summed(t, c, h, k).astype(BF16)
                src = part[c].at[h, 0, k]
                if k == 0:
                    rcopy(t, c, h, src, 12, 8, along(h, False, 1 + 2 * c)).start()
                elif k == 1 and c == 1:
                    rcopy(t, c, h, src, 13, 9, along(h, False, 1)).start()
                elif k == 3 and c == 0:
                    rcopy(t, c, h, src, 14, 9, along(h, False, 3)).start()

    def rs_merge2(t, c):
        k = 1 if c == 0 else 3
        for h in (0, 1):
            rcopy(t, c, h, rs[c].at[t % 2, h, 12], 12, 8, sib).wait_recv()
            got = rs[c][t % 2, h, 12].astype(F32)
            part[c][h, 0, k] = (part[c][h, 0, k].astype(F32) + got).astype(BF16)
            rcopy(t, c, h, part[c].at[h, 0, k], 13 + c, 9, along(h, False, k)).start()

    def rs_final(t, c, h):
        carried = summed(t, c, h, 2) + both_arrived(t, c, h, 13, 9)
        return em[t - 1, h, ROWS[c]].astype(F32) * carried

    def rs_sent(t, c):
        for h in (0, 1):
            every = rs[c].at[t % 2, h]
            remote(every, every, rs_send.at[c, h], rs_recv.at[t % 2, c, h, 0], sib).wait_send()

    def keep(t, c, h, weighted):
        states_of(t, c)[row * 2 + h] = weighted.astype(BF16)
        ag_start(t, c, h)

    def finish(t, c):
        if t < STEPS:
            ag_sent(t - 1, c)
        for h in (0, 1):
            weighted = rs_final(t, c, h)
            if t == STEPS:
                wfin[h, ROWS[c]] = weighted
            else:
                keep(t, c, h, weighted)

    def begin(t, c):
        ag_end(t - 1, c)
        if t > 1:
            rs_sent(t - 1, c)
        rs_multiply(t, c)

    def store_emitted(t):
        for h in (0, 1):
            em[t - 1, h] = e_final(t, h).astype(BF16)

    e_phase2(0)
    e_phase1(1)
    for h in (0, 1):
        first = e_final(0, h)
        for c in (0, 1):
            keep(0, c, h, first[ROWS[c]])
    for c in (0, 1):
        ag_relay1(0, c)
    for c in (0, 1):
        ag_relay2(0, c)
    blocks_copy().wait()
    for t in range(1, STEPS + 1):
        begin(t, 0)
        if t > 1:
            finish(t - 1, 1)
        rs_merge(t, 0)
        if t > 1:
            ag_relay1(t - 1, 1)
        rs_second(t, 0)
        if t > 1:
            ag_relay2(t - 1, 1)
        e_phase2(t)
        rs_merge2(t, 0)
        begin(t, 1)
        store_emitted(t)
        finish(t, 0)
        rs_merge(t, 1)
        if t < STEPS:
            e_phase1(t + 1)
            ag_relay1(t, 0)
        rs_second(t, 1)
        if t < STEPS:
            ag_relay2(t, 0)
        rs_merge2(t, 1)
    finish(STEPS, 1)

    wide = iota((SEQS, 128), 0) == iota((SEQS, 128), 1)
    total = jnp.sum(wfin[0] + wfin[1], axis=1, keepdims=True)
    mine = jnp.sum(jnp.where(wide, total, 0.0), axis=0, keepdims=True)
    ar0[0] = jnp.broadcast_to(mine, (8, 128))
    ar1[row] = ar0[0]

    def a1(i):
        return remote(ar0.at[0], ar1.at[row], a_send.at[0], a_recv.at[0], row_peers[i - 1])

    def a2(i):
        return remote(ar0.at[1], ar2.at[col], a_send.at[1], a_recv.at[1], col_peers[i - 1])

    seven = remote(ar1.at[0:7], ar1.at[0:7], a_send.at[0], a_recv.at[0], sib)
    fifteen = remote(ar2.at[0:15], ar2.at[0:15], a_send.at[1], a_recv.at[1], sib)
    for i in range(1, 8):
        a1(i).start()
    seven.wait_recv()
    ar0[1] = jnp.sum(ar1[...], axis=0)
    ar2[col] = ar0[1]
    for i in range(1, 16):
        a2(i).start()
    fifteen.wait_recv()
    scale = jnp.sum(ar2[...], axis=0)[0:1] * (1.0 / STATES)
    log_ref[...] = jnp.log(scale)
    scale_col = jnp.sum(jnp.where(wide, scale, 0.0), axis=1, keepdims=True)
    for h in (0, 1):
        post_ref[:, h * BLOCK : (h + 1) * BLOCK] = (wfin[h] / scale_col).astype(BF16)

    for c in (0, 1):
        rs_sent(STEPS, c)
        ag_sent(STEPS - 1, c)
    for t in range(STEPS + 1):
        remote(pack.at[t], pack.at[t], e_send.at[t, 0], e_recv.at[t, 0, 0], sib).wait_send()
        remote(pack.at[t], pack.at[t], e_send.at[t, 1], e_recv.at[t, 0, 0], sib).wait_send()
    seven.wait_send()
    fifteen.wait_send()


def on_device(blocks, source_ids, emission, tokens):
    vocab = emission.shape[0]
    dma = pltpu.SemaphoreType.DMA
    vmem = pltpu.VMEM
    posterior, logs = pl.pallas_call(
        kernel,
        out_shape=(jax.ShapeDtypeStruct((SEQS, 2 * BLOCK), BF16), jax.ShapeDtypeStruct((1, 128), F32)),
        in_specs=[
            pl.BlockSpec(memory_space=pltpu.SMEM),
            pl.BlockSpec(memory_space=pltpu.VMEM),
            pl.BlockSpec(memory_space=pl.ANY),
            pl.BlockSpec(memory_space=pl.ANY),
        ],
        out_specs=(pl.BlockSpec(memory_space=pltpu.VMEM), pl.BlockSpec(memory_space=pltpu.VMEM)),
        scratch_shapes=[
            vmem((32, BLOCK, BLOCK), BF16),
            vmem((32, vocab, BLOCK), BF16),
            vmem((4 * SLOT, vocab), BF16),
            vmem((STEPS + 1, 2, 3, 4, SLOT, BLOCK), BF16),
            vmem((STEPS + 1, 2, 4, 4, SLOT, BLOCK), BF16),
            vmem((STEPS + 1, 2, 4, 4, SLOT, BLOCK), BF16),
            vmem((STEPS, 2, SEQS, BLOCK), BF16),
            vmem((16, 48, BLOCK), BF16),
            vmem((16, 48, BLOCK), BF16),
            vmem((16, 56, BLOCK), BF16),
            vmem((16, 56, BLOCK), BF16),
            vmem((2, 4, 4, 48, BLOCK), BF16),
            vmem((2, 4, 4, 56, BLOCK), BF16),
            vmem((2, 2, 15, 48, BLOCK), BF16),
            vmem((2, 2, 15, 56, BLOCK), BF16),
            vmem((2, SEQS, BLOCK), F32),
            vmem((2, 8, 128), F32),
            vmem((8, 8, 128), F32),
            vmem((16, 8, 128), F32),
            dma,
            dma((32,)),
            dma((STEPS + 1, 2)),
            dma((STEPS + 1, 2, 2)),
            dma((2, 2)),
            dma((2, 2, 2, 4)),
            dma((2, 2)),
            dma((2, 2, 2, 10)),
            dma((2,)),
            dma((2,)),
        ],
        compiler_params=pltpu.CompilerParams(
            collective_id=0, has_side_effects=True, vmem_limit_bytes=63 * 2**20
        ),
        name="forward",
    )(source_ids.reshape(-1), tokens, blocks.reshape(32, BLOCK, BLOCK), emission)
    return posterior, logs[0, :SEQS]


def solution(mesh):
    in_specs = (P("row", "col", None, None), P("row", "col"), P("col", "row"), P())
    out_specs = (P(None, ("row", "col")), P())
    return jax.shard_map(on_device, mesh=mesh, in_specs=in_specs, out_specs=out_specs, check_vma=False)
```

time: 162 us -> 151 us (0.932)
  Pallas kernels: 158 us -> 148 us
    pallas_call x1, Pallas kernels: 158 us -> 148 us  [on_device(): pl.pallas_call(kernel, out_shape=(jax.ShapeDtypeStruct((SEQS, 2 * BLOCK),...]
where the time goes in v2:
time: 151 us
  Pallas kernels  148 us (98%)
  local copies, waits for them, and re-layouts  2.74 us (2%)
    pallas_call x1, Pallas kernels, on_device(): pl.pallas_call(kernel, out_shape=(jax.ShapeDtypeStruct((SEQS, 2 * BLOCK),...  148 us

profile of v2, /device:TPU:1, one launch (start us, length us, event | category | flops | bytes accessed | tf_op | source)
XLA Modules:
  0.0 151.2 jit_solution(1540227447551385767)
XLA Ops:
  0.6 147.8 %forward.1 = (bf16[104,1024]{1,0:T(8,128)(2,1)}, f32[1,128]{1,0:T(1,128)}) custom-call(s32[32]{0:T(128)} %bitcast.5, s32[4,104]{1,0:T(4,128)} %tok_ref.1, bf16[32,512,512]{2,1,0:T(8,128)(2,1)} %bitcast.4, bf16[313,16384]{1,0:T(8,128)(2,1)} %emis_hbm.1), custom_call_target="tpu_custom_call" | custom-call | tf_op jit(solution)/shard_map/forward/pallas_call | solution.py:415
  148.4 1.1 slice_bitcast_fusion
  149.6 1.6 %copy.7 = bf16[104,1024]{1,0:T(8,128)(2,1)} copy(bf16[104,1024]{1,0:T(8,128)(2,1)} %get-tuple-element.8) | data formatting | bytes 425984

commit v3 on v2

--- a/solution.py
+++ b/solution.py
@@ -24,8 +24,8 @@
 
 
 def kernel(
-    ids_ref, tok_ref, blocks_hbm, emis_hbm, post_ref, log_ref,
-    blocks_v, emis_v, sel_v, pack, land1, land2, em, states_a, states_b, states_c, states_d, part_a, part_b, rs_a, rs_b, wfin, ar0, ar1, ar2,
+    ids_ref, tok_ref, blocks_hbm, emis_hbm, wfin, scale_ref,
+    blocks_v, emis_v, sel_v, pack, land1, land2, em, states_a, states_b, states_c, states_d, part_a, part_b, rs_a, rs_b, ar0, ar1, ar2,
     blk_sem, emis_sem, e_send, e_recv, ag_send, ag_recv, rs_send, rs_recv, a_send, a_recv,
 ):
     row = lax.axis_index("row")
@@ -108,8 +108,6 @@
         id_of = jnp.where(to_col(tok_row) - me * float(vocab) == iota((SEQS, vocab), 1), 1.0, 0.0).astype(BF16)
         sel_v[t * SLOT : (t + 1) * SLOT, :] = jnp.dot(slot_of, id_of, preferred_element_type=F32).astype(BF16)
 
-    pl.semaphore_wait(barrier, 22)
-
     def e1(t, h, po):
         p, _ = pq(h)
         return remote(
@@ -127,9 +125,7 @@
     for po in (2, 1, 3, 0):
         for h in (0, 1):
             p, _ = pq(h)
-
-            @pl.loop(0, 4)
-            def _(qd):
+            for qd in range(4):
                 chunk = chunk_of(h, po, qd)
                 emis_copy(chunk).wait()
                 rows = jnp.dot(sel_v[...], emis_v[chunk], preferred_element_type=F32).astype(BF16)
@@ -139,7 +135,8 @@
                         pack[t, h, po - 1, qd] = piece
                     else:
                         land1[t, h, qd, p] = piece
-
+            if po == 2 and h == 0:
+                pl.semaphore_wait(barrier, 22)
             if po:
                 e1(0, h, po).start()
 
@@ -183,24 +180,16 @@
         return ((y + off) % 4) * 2 + core
 
     def ag_start(t, c, h):
-        ag(t, c, h, row, 0, at_y(1)).start()
-        ag(t, c, h, row, 1, at_y(3)).start()
+        for sem, off in enumerate((1, 3, 2)):
+            ag(t, c, h, row, sem, at_y(off)).start()
         ag(t, c, h, row, 3, sib).start()
 
-    def ag_relay1(t, c):
-        for sem, off, on in ((0, 3, 1), (1, 1, 3)):
+    def ag_relay(t, c, sems):
+        for sem in sems:
             for h in (0, 1):
-                of = same_core(off)
+                of = same_core((3, 1, 2)[sem])
                 ag(t, c, h, of, sem, sib).wait_recv()
-                if sem == h:
-                    ag(t, c, h, of, 2, at_y(on)).start()
                 ag(t, c, h, of, 3, sib).start()
-
-    def ag_relay2(t, c):
-        for h in (0, 1):
-            of = same_core(2)
-            ag(t, c, h, of, 2, sib).wait_recv()
-            ag(t, c, h, of, 3, sib).start()
 
     def ag_end(t, c):
         for h in (0, 1):
@@ -229,10 +218,10 @@
         rcopy(t, c, h, rs[c].at[t % 2, h, k], k, k, sib).wait_recv()
         return rs[c][t % 2, h, k].astype(F32)
 
-    def both_arrived(t, c, h, msg, sem):
-        pair = rs[c].at[t % 2, h, pl.ds(msg, 2)]
-        remote(pair, pair, rs_send.at[c, h], rs_recv.at[t % 2, c, h, sem], sib).wait_recv()
-        return rs[c][t % 2, h, msg].astype(F32) + rs[c][t % 2, h, msg + 1].astype(F32)
+    def arrived_in(t, c, h, msg, count, sem):
+        items = rs[c].at[t % 2, h, pl.ds(msg, count)]
+        remote(items, items, rs_send.at[c, h], rs_recv.at[t % 2, c, h, sem], sib).wait_recv()
+        return sum(rs[c][t % 2, h, msg + i].astype(F32) for i in range(count))
 
     def rs_multiply(t, c):
         @pl.loop(0, 2)
@@ -279,30 +268,16 @@
                     rcopy(t, c, h, part[c].at[h, po, k2], 4 + 2 * k2 + k, 4 + k2, along(h, True, po)).start()
 
     def summed(t, c, h, k):
-        return part[c][h, 0, k].astype(F32) + both_arrived(t, c, h, 4 + 2 * k, 4 + k)
+        return part[c][h, 0, k].astype(F32) + arrived_in(t, c, h, 4 + 2 * k, 2, 4 + k)
 
     def rs_second(t, c):
-        for k in (0, 1, 3):
+        for k, msg, off in ((0, 12, 2), (1, 13, 1), (3, 14, 3)):
             for h in (0, 1):
                 part[c][h, 0, k] = summed(t, c, h, k).astype(BF16)
-                src = part[c].at[h, 0, k]
-                if k == 0:
-                    rcopy(t, c, h, src, 12, 8, along(h, False, 1 + 2 * c)).start()
-                elif k == 1 and c == 1:
-                    rcopy(t, c, h, src, 13, 9, along(h, False, 1)).start()
-                elif k == 3 and c == 0:
-                    rcopy(t, c, h, src, 14, 9, along(h, False, 3)).start()
-
-    def rs_merge2(t, c):
-        k = 1 if c == 0 else 3
-        for h in (0, 1):
-            rcopy(t, c, h, rs[c].at[t % 2, h, 12], 12, 8, sib).wait_recv()
-            got = rs[c][t % 2, h, 12].astype(F32)
-            part[c][h, 0, k] = (part[c][h, 0, k].astype(F32) + got).astype(BF16)
-            rcopy(t, c, h, part[c].at[h, 0, k], 13 + c, 9, along(h, False, k)).start()
+                rcopy(t, c, h, part[c].at[h, 0, k], msg, 8, along(h, False, off)).start()
 
     def rs_final(t, c, h):
-        carried = summed(t, c, h, 2) + both_arrived(t, c, h, 13, 9)
+        carried = summed(t, c, h, 2) + arrived_in(t, c, h, 12, 3, 8)
         return em[t - 1, h, ROWS[c]].astype(F32) * carried
 
     def rs_sent(t, c):
@@ -320,7 +295,7 @@
         for h in (0, 1):
             weighted = rs_final(t, c, h)
             if t == STEPS:
-                wfin[h, ROWS[c]] = weighted
+                wfin[ROWS[c], h * BLOCK : (h + 1) * BLOCK] = weighted
             else:
                 keep(t, c, h, weighted)
 
@@ -341,9 +316,7 @@
         for c in (0, 1):
             keep(0, c, h, first[ROWS[c]])
     for c in (0, 1):
-        ag_relay1(0, c)
-    for c in (0, 1):
-        ag_relay2(0, c)
+        ag_relay(0, c, (0, 1, 2))
     blocks_copy().wait()
     for t in range(1, STEPS + 1):
         begin(t, 0)
@@ -351,27 +324,25 @@
             finish(t - 1, 1)
         rs_merge(t, 0)
         if t > 1:
-            ag_relay1(t - 1, 1)
+            ag_relay(t - 1, 1, (0, 1))
         rs_second(t, 0)
         if t > 1:
-            ag_relay2(t - 1, 1)
+            ag_relay(t - 1, 1, (2,))
         e_phase2(t)
-        rs_merge2(t, 0)
         begin(t, 1)
         store_emitted(t)
         finish(t, 0)
         rs_merge(t, 1)
         if t < STEPS:
             e_phase1(t + 1)
-            ag_relay1(t, 0)
+            ag_relay(t, 0, (0, 1))
         rs_second(t, 1)
         if t < STEPS:
-            ag_relay2(t, 0)
-        rs_merge2(t, 1)
+            ag_relay(t, 0, (2,))
     finish(STEPS, 1)
 
     wide = iota((SEQS, 128), 0) == iota((SEQS, 128), 1)
-    total = jnp.sum(wfin[0] + wfin[1], axis=1, keepdims=True)
+    total = jnp.sum(wfin[:, :BLOCK] + wfin[:, BLOCK:], axis=1, keepdims=True)
     mine = jnp.sum(jnp.where(wide, total, 0.0), axis=0, keepdims=True)
     ar0[0] = jnp.broadcast_to(mine, (8, 128))
     ar1[row] = ar0[0]
@@ -392,11 +363,7 @@
     for i in range(1, 16):
         a2(i).start()
     fifteen.wait_recv()
-    scale = jnp.sum(ar2[...], axis=0)[0:1] * (1.0 / STATES)
-    log_ref[...] = jnp.log(scale)
-    scale_col = jnp.sum(jnp.where(wide, scale, 0.0), axis=1, keepdims=True)
-    for h in (0, 1):
-        post_ref[:, h * BLOCK : (h + 1) * BLOCK] = (wfin[h] / scale_col).astype(BF16)
+    scale_ref[...] = jnp.sum(ar2[...], axis=0) * (1.0 / STATES)
 
     for c in (0, 1):
         rs_sent(STEPS, c)
@@ -408,13 +375,21 @@
     fifteen.wait_send()
 
 
+def normalize(weights_ref, scale_ref, post_ref, log_ref):
+    wide = iota((SEQS, 128), 0) == iota((SEQS, 128), 1)
+    scale = scale_ref[0:1, :]
+    log_ref[...] = jnp.log(scale[:, :SEQS])
+    scale_col = jnp.sum(jnp.where(wide, scale, 0.0), axis=1, keepdims=True)
+    post_ref[...] = (weights_ref[...] / scale_col).astype(BF16)
+
+
 def on_device(blocks, source_ids, emission, tokens):
     vocab = emission.shape[0]
     dma = pltpu.SemaphoreType.DMA
     vmem = pltpu.VMEM
-    posterior, logs = pl.pallas_call(
+    weights, scale = pl.pallas_call(
         kernel,
-        out_shape=(jax.ShapeDtypeStruct((SEQS, 2 * BLOCK), BF16), jax.ShapeDtypeStruct((1, 128), F32)),
+        out_shape=(jax.ShapeDtypeStruct((SEQS, 2 * BLOCK), F32), jax.ShapeDtypeStruct((8, 128), F32)),
         in_specs=[
             pl.BlockSpec(memory_space=pltpu.SMEM),
             pl.BlockSpec(memory_space=pltpu.VMEM),
@@ -438,7 +413,6 @@
             vmem((2, 4, 4, 56, BLOCK), BF16),
             vmem((2, 2, 15, 48, BLOCK), BF16),
             vmem((2, 2, 15, 56, BLOCK), BF16),
-            vmem((2, SEQS, BLOCK), F32),
             vmem((2, 8, 128), F32),
             vmem((8, 8, 128), F32),
             vmem((16, 8, 128), F32),
@@ -449,7 +423,7 @@
             dma((2, 2)),
             dma((2, 2, 2, 4)),
             dma((2, 2)),
-            dma((2, 2, 2, 10)),
+            dma((2, 2, 2, 9)),
             dma((2,)),
             dma((2,)),
         ],
@@ -458,7 +432,14 @@
         ),
         name="forward",
     )(source_ids.reshape(-1), tokens, blocks.reshape(32, BLOCK, BLOCK), emission)
-    return posterior, logs[0, :SEQS]
+    posterior, logs = pl.pallas_call(
+        normalize,
+        out_shape=(jax.ShapeDtypeStruct((SEQS, 2 * BLOCK), BF16), jax.ShapeDtypeStruct((1, SEQS), F32)),
+        in_specs=[pl.BlockSpec(memory_space=pltpu.VMEM)] * 2,
+        out_specs=(pl.BlockSpec(memory_space=pltpu.VMEM), pl.BlockSpec(memory_space=pltpu.VMEM)),
+        name="normalize",
+    )(weights, scale)
+    return posterior, logs.reshape(SEQS)
 
 
 def solution(mesh):

time: 151 us -> 145 us (0.960)
  Pallas kernels: 148 us -> 144 us
  local copies, waits for them, and re-layouts: 2.74 us -> 0 us
    pallas_call x1, Pallas kernels: 148 us -> 143 us  [on_device(): pl.pallas_call(kernel, out_shape=(jax.ShapeDtypeStruct((SEQS, 2 * BLOCK),...]
    pallas_call x0 -> x1, Pallas kernels: none -> 1.8 us  [on_device(): pl.pallas_call(normalize, out_shape=(jax.ShapeDtypeStruct((SEQS, 2 * BLOC...]
    unnamed x1 -> x0, local copies, waits for them, and re-layouts: 1.63 us -> none
where the time goes in v3:
time: 145 us
  Pallas kernels  144 us (99%)
    pallas_call x1, Pallas kernels, on_device(): pl.pallas_call(kernel, out_shape=(jax.ShapeDtypeStruct((SEQS, 2 * BLOCK),...  143 us

profile of v3, /device:TPU:1, one launch (start us, length us, event | category | flops | bytes accessed | tf_op | source)
XLA Modules:
  0.0 145.0 jit_solution(54649066261252268)
XLA Ops:
  0.6 142.6 %forward.1 = (f32[104,1024]{1,0:T(8,128)}, f32[8,128]{1,0:T(8,128)}) custom-call(s32[32]{0:T(128)} %bitcast.4, s32[4,104]{1,0:T(4,128)} %tok_ref.1, bf16[32,512,512]{2,1,0:T(8,128)(2,1)} %bitcast.3, bf16[313,16384]{1,0:T(8,128)(2,1)} %emis_hbm.1), custom_call_target="tpu_custom_call" | custom-call | tf_op jit(solution)/shard_map/forward/pallas_call | solution.py:390
  143.2 1.8 %normalize.1 = (bf16[104,1024]{1,0:T(8,128)(2,1)}, f32[1,104]{1,0:T(1,128)}) custom-call(f32[104,1024]{1,0:T(8,128)} %get-tuple-element.6.weights_ref, f32[8,128]{1,0:T(8,128)} %get-tuple-element.7.scale_ref), custom_call_target="tpu_custom_call" | custom-call | tf_op jit(solution)/shard_map/normalize/pallas_call | solution.py:435

commit v4 on v3

--- a/solution.py
+++ b/solution.py
@@ -25,8 +25,8 @@
 
 def kernel(
     ids_ref, tok_ref, blocks_hbm, emis_hbm, wfin, scale_ref,
-    blocks_v, emis_v, sel_v, pack, land1, land2, em, states_a, states_b, states_c, states_d, part_a, part_b, rs_a, rs_b, ar0, ar1, ar2,
-    blk_sem, emis_sem, e_send, e_recv, ag_send, ag_recv, rs_send, rs_recv, a_send, a_recv,
+    blocks_v, emis_v, sel_v, pack, land1, land2_a, land2_b, mid_a, mid_b, own, em, states_a, states_b, states_c, states_d, part_a, part_b, rs_a, rs_b, ar0, ar1, ar2,
+    blk_sem, emis_sem, e_send, e_recv, e_send2, e_recv2, ag_send, ag_recv, rs_send, rs_recv, a_send, a_recv,
 ):
     row = lax.axis_index("row")
     col = lax.axis_index("col")
@@ -34,6 +34,8 @@
     x, z = col // 4, col % 4
     vocab = emis_v.shape[1]
     states = (states_a, states_b, states_c, states_d)
+    land2 = (land2_a, land2_b)
+    mid = (mid_a, mid_b)
     part = (part_a, part_b)
     rs = (rs_a, rs_b)
 
@@ -111,15 +113,13 @@
     def e1(t, h, po):
         p, _ = pq(h)
         return remote(
-            pack.at[t, h, po - 1], land1.at[t, h, :, p], e_send.at[t, 0], e_recv.at[t, 0, h],
+            pack.at[t, h, po - 1], land1.at[t, h, :, p], e_send.at[t], e_recv.at[t, h],
             along(h, True, po),
         )
 
-    def e2(t, h, qo):
-        _, q = pq(h)
+    def e2(t, c, h, qo):
         return remote(
-            land1.at[t, h, (q + qo) % 4], land2.at[t, h, q], e_send.at[t, 1], e_recv.at[t, 1, h],
-            along(h, False, qo),
+            mid[c].at[h, qo - 1], land2[c].at[t, h, qo - 1], e_send2.at[c], e_recv2.at[t, c, h], along(h, False, qo)
         )
 
     for po in (2, 1, 3, 0):
@@ -140,34 +140,44 @@
             if po:
                 e1(0, h, po).start()
 
-    def e_phase1(t):
-        for po in (2, 1, 3):
-            for h in (0, 1):
-                e1(t, h, po).start()
-
-    def e_phase2(t):
-        for h in (0, 1):
-            three = land1.at[t, h, :, 0:3]
-            remote(three, three, e_send.at[t, 0], e_recv.at[t, 0, h], sib).wait_recv()
-            for qo in (2, 1, 3):
-                e2(t, h, qo).start()
-
-    def e_final(t, h):
-        p, q = pq(h)
-        land2[t, h, q] = land1[t, h, q]
+    def e_first(t, po):
+        for h in (0, 1):
+            e1(t, h, po).start()
+
+    def e_sent2():
+        for c in (0, 1):
+            remote(mid[c], mid[c], e_send2.at[c], e_recv2.at[0, c, 0], sib).wait_send()
+
+    def e_middle(t, h):
+        _, q = pq(h)
         _, _, owner_col, pos_row = places(t)
-        if h == 0:
-            high = jnp.zeros_like(owner_col)
-            for k in range(1, 4):
-                high += jnp.where(owner_col >= float(4 * k), 1.0, 0.0)
-            place = (owner_col - 4.0 * high) * 4.0 + high
-        else:
-            place = owner_col
-        target = place * float(SLOT) + to_col(pos_row)
-        pick = jnp.where(iota((SEQS, 16 * SLOT), 1) == target, 1.0, 0.0).astype(BF16)
-        three = land2.at[t, h, 0:3]
-        remote(three, three, e_send.at[t, 1], e_recv.at[t, 1, h], sib).wait_recv()
-        return jnp.dot(pick, land2[t, h].reshape(16 * SLOT, BLOCK), preferred_element_type=F32)
+        x_of = jnp.zeros_like(owner_col)
+        for k in range(1, 4):
+            x_of += jnp.where(owner_col >= float(4 * k), 1.0, 0.0)
+        z_of = owner_col - 4.0 * x_of
+        p_of, q_of = (x_of, z_of) if h == 0 else (z_of, x_of)
+        place = p_of * float(SLOT) + to_col(pos_row)
+        lane = iota((SEQS, 4 * SLOT), 1)
+        pick = jnp.where((lane == place) & (q_of == q.astype(F32)), 1.0, 0.0).astype(BF16)
+        three = land1.at[t, h, :, 0:3]
+        remote(three, three, e_send.at[t], e_recv.at[t, h], sib).wait_recv()
+        for qo in (2, 1, 3, 0):
+            packed = land1[t, h, (q + qo) % 4].reshape(4 * SLOT, BLOCK)
+            rows = jnp.dot(pick, packed, preferred_element_type=F32).astype(BF16)
+            if qo:
+                for c in (0, 1):
+                    mid[c][h, qo - 1] = rows[ROWS[c]]
+            else:
+                own[h] = rows
+
+    def e_second(t, c, h):
+        for qo in (2, 1, 3):
+            e2(t, c, h, qo).start()
+
+    def e_final(t, c, h):
+        three = land2[c].at[t, h]
+        remote(three, three, e_send2.at[c], e_recv2.at[t, c, h], sib).wait_recv()
+        return own[h, ROWS[c]].astype(F32) + sum(land2[c][t, h, i].astype(F32) for i in range(3))
 
     def states_of(t, c):
         return states[c * 2 + t % 2]
@@ -305,21 +315,49 @@
             rs_sent(t - 1, c)
         rs_multiply(t, c)
 
-    def store_emitted(t):
-        for h in (0, 1):
-            em[t - 1, h] = e_final(t, h).astype(BF16)
-
-    e_phase2(0)
-    e_phase1(1)
+    def store_emitted(t, c):
+        for h in (0, 1):
+            em[t - 1, h, ROWS[c]] = e_final(t, c, h).astype(BF16)
+
     for h in (0, 1):
-        first = e_final(0, h)
-        for c in (0, 1):
-            keep(0, c, h, first[ROWS[c]])
+        e_middle(0, h)
+        e_second(0, 0, h)
+    for h in (0, 1):
+        e_second(0, 1, h)
+    for po in (2, 1, 3):
+        e_first(1, po)
+    for c in (0, 1):
+        for h in (0, 1):
+            keep(0, c, h, e_final(0, c, h))
     for c in (0, 1):
         ag_relay(0, c, (0, 1, 2))
+    e_sent2()
+    for h in (0, 1):
+        e_middle(1, h)
     blocks_copy().wait()
+
+    def emission(t, slot):
+        if t == STEPS:
+            return
+        if slot < 3:
+            e_first(t + 1, (2, 1, 3)[slot])
+        elif slot == 3:
+            e_sent2()
+            e_middle(t + 1, 0)
+            e_second(t + 1, 0, 0)
+        elif slot == 4:
+            e_middle(t + 1, 1)
+            e_second(t + 1, 0, 1)
+        else:
+            for h in (0, 1):
+                e_second(t + 1, 1, h)
+
     for t in range(1, STEPS + 1):
         begin(t, 0)
+        if t == 1:
+            for c in (0, 1):
+                for h in (0, 1):
+                    e_second(1, c, h)
         if t > 1:
             finish(t - 1, 1)
         rs_merge(t, 0)
@@ -328,15 +366,20 @@
         rs_second(t, 0)
         if t > 1:
             ag_relay(t - 1, 1, (2,))
-        e_phase2(t)
         begin(t, 1)
-        store_emitted(t)
+        emission(t, 0)
+        emission(t, 1)
+        emission(t, 2)
+        store_emitted(t, 0)
+        store_emitted(t, 1)
         finish(t, 0)
         rs_merge(t, 1)
         if t < STEPS:
-            e_phase1(t + 1)
             ag_relay(t, 0, (0, 1))
         rs_second(t, 1)
+        emission(t, 3)
+        emission(t, 4)
+        emission(t, 5)
         if t < STEPS:
             ag_relay(t, 0, (2,))
     finish(STEPS, 1)
@@ -368,9 +411,9 @@
     for c in (0, 1):
         rs_sent(STEPS, c)
         ag_sent(STEPS - 1, c)
+    e_sent2()
     for t in range(STEPS + 1):
-        remote(pack.at[t], pack.at[t], e_send.at[t, 0], e_recv.at[t, 0, 0], sib).wait_send()
-        remote(pack.at[t], pack.at[t], e_send.at[t, 1], e_recv.at[t, 0, 0], sib).wait_send()
+        remote(pack.at[t], pack.at[t], e_send.at[t], e_recv.at[t, 0], sib).wait_send()
     seven.wait_send()
     fifteen.wait_send()
 
@@ -403,7 +446,11 @@
             vmem((4 * SLOT, vocab), BF16),
             vmem((STEPS + 1, 2, 3, 4, SLOT, BLOCK), BF16),
             vmem((STEPS + 1, 2, 4, 4, SLOT, BLOCK), BF16),
-            vmem((STEPS + 1, 2, 4, 4, SLOT, BLOCK), BF16),
+            vmem((STEPS + 1, 2, 3, 48, BLOCK), BF16),
+            vmem((STEPS + 1, 2, 3, 56, BLOCK), BF16),
+            vmem((2, 3, 48, BLOCK), BF16),
+            vmem((2, 3, 56, BLOCK), BF16),
+            vmem((2, SEQS, BLOCK), BF16),
             vmem((STEPS, 2, SEQS, BLOCK), BF16),
             vmem((16, 48, BLOCK), BF16),
             vmem((16, 48, BLOCK), BF16),
@@ -418,7 +465,9 @@
             vmem((16, 8, 128), F32),
             dma,
             dma((32,)),
+            dma((STEPS + 1,)),
             dma((STEPS + 1, 2)),
+            dma((2,)),
             dma((STEPS + 1, 2, 2)),
             dma((2, 2)),
             dma((2, 2, 2, 4)),

time: 145 us -> 137 us (0.945)
  Pallas kernels: 144 us -> 137 us
    pallas_call x1, Pallas kernels: 143 us -> 135 us  [on_device(): pl.pallas_call(kernel, out_shape=(jax.ShapeDtypeStruct((SEQS, 2 * BLOCK),...]
where the time goes in v4:
time: 137 us
  Pallas kernels  137 us (100%)
    pallas_call x1, Pallas kernels, on_device(): pl.pallas_call(kernel, out_shape=(jax.ShapeDtypeStruct((SEQS, 2 * BLOCK),...  135 us

profile of v4, /device:TPU:1, one launch (start us, length us, event | category | flops | bytes accessed | tf_op | source)
XLA Modules:
  0.0 137.2 jit_solution(15615254877494899404)
XLA Ops:
  0.6 134.7 %forward.1 = (f32[104,1024]{1,0:T(8,128)}, f32[8,128]{1,0:T(8,128)}) custom-call(s32[32]{0:T(128)} %bitcast.4, s32[4,104]{1,0:T(4,128)} %tok_ref.1, bf16[32,512,512]{2,1,0:T(8,128)(2,1)} %bitcast.3, bf16[313,16384]{1,0:T(8,128)(2,1)} %emis_hbm.1), custom_call_target="tpu_custom_call" | custom-call | tf_op jit(solution)/shard_map/forward/pallas_call | solution.py:433
  135.4 1.8 %normalize.1 = (bf16[104,1024]{1,0:T(8,128)(2,1)}, f32[1,104]{1,0:T(1,128)}) custom-call(f32[104,1024]{1,0:T(8,128)} %get-tuple-element.6.weights_ref, f32[8,128]{1,0:T(8,128)} %get-tuple-element.7.scale_ref), custom_call_target="tpu_custom_call" | custom-call | tf_op jit(solution)/shard_map/normalize/pallas_call | solution.py:484

commit v5 on v4

--- a/solution.py
+++ b/solution.py
@@ -331,57 +331,44 @@
             keep(0, c, h, e_final(0, c, h))
     for c in (0, 1):
         ag_relay(0, c, (0, 1, 2))
-    e_sent2()
-    for h in (0, 1):
-        e_middle(1, h)
     blocks_copy().wait()
 
-    def emission(t, slot):
-        if t == STEPS:
+    def emission(t, part):
+        if t > STEPS:
             return
-        if slot < 3:
-            e_first(t + 1, (2, 1, 3)[slot])
-        elif slot == 3:
-            e_sent2()
-            e_middle(t + 1, 0)
-            e_second(t + 1, 0, 0)
-        elif slot == 4:
-            e_middle(t + 1, 1)
-            e_second(t + 1, 0, 1)
+        if part < 3:
+            e_first(t, (2, 1, 3)[part])
+        elif part < 5:
+            if part == 3:
+                e_sent2()
+            e_middle(t, part - 3)
+            e_second(t, 0, part - 3)
         else:
             for h in (0, 1):
-                e_second(t + 1, 1, h)
+                e_second(t, 1, h)
 
     for t in range(1, STEPS + 1):
         begin(t, 0)
-        if t == 1:
-            for c in (0, 1):
-                for h in (0, 1):
-                    e_second(1, c, h)
+        emission(t, 3)
+        emission(t, 4)
         if t > 1:
             finish(t - 1, 1)
         rs_merge(t, 0)
+        emission(t, 5)
         if t > 1:
-            ag_relay(t - 1, 1, (0, 1))
+            ag_relay(t - 1, 1, (0, 1, 2))
         rs_second(t, 0)
-        if t > 1:
-            ag_relay(t - 1, 1, (2,))
         begin(t, 1)
-        emission(t, 0)
-        emission(t, 1)
-        emission(t, 2)
         store_emitted(t, 0)
+        finish(t, 0)
+        emission(t + 1, 0)
+        emission(t + 1, 1)
+        rs_merge(t, 1)
+        emission(t + 1, 2)
+        if t < STEPS:
+            ag_relay(t, 0, (0, 1, 2))
+        rs_second(t, 1)
         store_emitted(t, 1)
-        finish(t, 0)
-        rs_merge(t, 1)
-        if t < STEPS:
-            ag_relay(t, 0, (0, 1))
-        rs_second(t, 1)
-        emission(t, 3)
-        emission(t, 4)
-        emission(t, 5)
-        if t < STEPS:
-            ag_relay(t, 0, (2,))
     finish(STEPS, 1)
 
     wide = iota((SEQS, 128), 0) == iota((SEQS, 128), 1)

time: 137 us -> 132 us (0.964)
  Pallas kernels: 137 us -> 131 us
    pallas_call x1, Pallas kernels: 135 us -> 129 us  [on_device(): pl.pallas_call(kernel, out_shape=(jax.ShapeDtypeStruct((SEQS, 2 * BLOCK),...]
where the time goes in v5:
time: 132 us; the launch traced here: 131 us
  Pallas kernels  131 us (99%)
    pallas_call x1, Pallas kernels, on_device(): pl.pallas_call(kernel, out_shape=(jax.ShapeDtypeStruct((SEQS, 2 * BLOCK),...  129 us

profile of v5, /device:TPU:1, one launch (start us, length us, event | category | flops | bytes accessed | tf_op | source)
XLA Modules:
  0.0 131.4 jit_solution(4538242040053849616)
XLA Ops:
  0.6 129.0 %forward.1 = (f32[104,1024]{1,0:T(8,128)}, f32[8,128]{1,0:T(8,128)}) custom-call(s32[32]{0:T(128)} %bitcast.4, s32[4,104]{1,0:T(4,128)} %tok_ref.1, bf16[32,512,512]{2,1,0:T(8,128)(2,1)} %bitcast.3, bf16[313,16384]{1,0:T(8,128)(2,1)} %emis_hbm.1), custom_call_target="tpu_custom_call" | custom-call | tf_op jit(solution)/shard_map/forward/pallas_call | solution.py:420
  129.6 1.8 %normalize.1 = (bf16[104,1024]{1,0:T(8,128)(2,1)}, f32[1,104]{1,0:T(1,128)}) custom-call(f32[104,1024]{1,0:T(8,128)} %get-tuple-element.6.weights_ref, f32[8,128]{1,0:T(8,128)} %get-tuple-element.7.scale_ref), custom_call_target="tpu_custom_call" | custom-call | tf_op jit(solution)/shard_map/normalize/pallas_call | solution.py:471

commit v6 on v5

--- a/solution.py
+++ b/solution.py
@@ -15,6 +15,7 @@
 BLOCK = 512
 STEPS = 3
 ROWS = (slice(0, 48), slice(48, 104))
+QOFF = (2, 1, 3, 0)
 F32 = jnp.float32
 BF16 = jnp.bfloat16
 
@@ -70,11 +71,16 @@
         pd = (p + po) % 4
         return (pd * 4 + qd) * 2 if h == 0 else (qd * 4 + pd) * 2 + 1
 
-    for po in (2, 1, 3, 0):
-        for h in (0, 1):
-            @pl.loop(0, 4)
-            def _(qd):
-                emis_copy(chunk_of(h, po, qd)).start()
+    groups = [(half, po) for half in (0, 1) for po in (2, 1, 3)] + [(0, 0), (1, 0)]
+
+    def chunks(half, po, h):
+        _, q = pq(h)
+        return [(i, chunk_of(h, po, (q + QOFF[i]) % 4)) for i in (2 * half, 2 * half + 1)]
+
+    for half, po in groups:
+        for h in (0, 1):
+            for _, chunk in chunks(half, po, h):
+                emis_copy(chunk).start()
 
     def blocks_copy():
         return pltpu.make_async_copy(blocks_hbm, blocks_v, blk_sem)
@@ -110,35 +116,38 @@
         id_of = jnp.where(to_col(tok_row) - me * float(vocab) == iota((SEQS, vocab), 1), 1.0, 0.0).astype(BF16)
         sel_v[t * SLOT : (t + 1) * SLOT, :] = jnp.dot(slot_of, id_of, preferred_element_type=F32).astype(BF16)
 
-    def e1(t, h, po):
+    def e1(t, h, po, part=slice(0, 4)):
         p, _ = pq(h)
         return remote(
-            pack.at[t, h, po - 1], land1.at[t, h, :, p], e_send.at[t], e_recv.at[t, h],
+            pack.at[t, h, po - 1, part], land1.at[t, h, part, p], e_send.at[t], e_recv.at[t, h, part.start // 2],
             along(h, True, po),
         )
+
+    def e1_arrived(t, h, part=slice(0, 4)):
+        three = land1.at[t, h, part, 0:3]
+        remote(three, three, e_send.at[t], e_recv.at[t, h, part.start // 2], sib).wait_recv()
 
     def e2(t, c, h, qo):
         return remote(
             mid[c].at[h, qo - 1], land2[c].at[t, h, qo - 1], e_send2.at[c], e_recv2.at[t, c, h], along(h, False, qo)
         )
 
-    for po in (2, 1, 3, 0):
+    for half, po in groups:
         for h in (0, 1):
             p, _ = pq(h)
-            for qd in range(4):
-                chunk = chunk_of(h, po, qd)
+            for i, chunk in chunks(half, po, h):
                 emis_copy(chunk).wait()
                 rows = jnp.dot(sel_v[...], emis_v[chunk], preferred_element_type=F32).astype(BF16)
                 for t in range(STEPS + 1):
                     piece = rows[t * SLOT : (t + 1) * SLOT]
                     if po:
-                        pack[t, h, po - 1, qd] = piece
+                        pack[t, h, po - 1, i] = piece
                     else:
-                        land1[t, h, qd, p] = piece
-            if po == 2 and h == 0:
+                        land1[t, h, i, p] = piece
+            if (half, po, h) == (0, 2, 0):
                 pl.semaphore_wait(barrier, 22)
             if po:
-                e1(0, h, po).start()
+                e1(0, h, po, slice(2 * half, 2 * half + 2)).start()
 
     def e_first(t, po):
         for h in (0, 1):
@@ -148,7 +157,7 @@
         for c in (0, 1):
             remote(mid[c], mid[c], e_send2.at[c], e_recv2.at[0, c, 0], sib).wait_send()
 
-    def e_middle(t, h):
+    def e_pick(t, h):
         _, q = pq(h)
         _, _, owner_col, pos_row = places(t)
         x_of = jnp.zeros_like(owner_col)
@@ -158,17 +167,21 @@
         p_of, q_of = (x_of, z_of) if h == 0 else (z_of, x_of)
         place = p_of * float(SLOT) + to_col(pos_row)
         lane = iota((SEQS, 4 * SLOT), 1)
-        pick = jnp.where((lane == place) & (q_of == q.astype(F32)), 1.0, 0.0).astype(BF16)
-        three = land1.at[t, h, :, 0:3]
-        remote(three, three, e_send.at[t], e_recv.at[t, h], sib).wait_recv()
-        for qo in (2, 1, 3, 0):
-            packed = land1[t, h, (q + qo) % 4].reshape(4 * SLOT, BLOCK)
-            rows = jnp.dot(pick, packed, preferred_element_type=F32).astype(BF16)
-            if qo:
-                for c in (0, 1):
-                    mid[c][h, qo - 1] = rows[ROWS[c]]
-            else:
-                own[h] = rows
+        return jnp.where((lane == place) & (q_of == q.astype(F32)), 1.0, 0.0).astype(BF16)
+
+    def e_place(t, h, pick, i):
+        rows = jnp.dot(pick, land1[t, h, i].reshape(4 * SLOT, BLOCK), preferred_element_type=F32).astype(BF16)
+        if QOFF[i]:
+            for c in (0, 1):
+                mid[c][h, QOFF[i] - 1] = rows[ROWS[c]]
+        else:
+            own[h] = rows
+
+    def e_middle(t, h):
+        pick = e_pick(t, h)
+        e1_arrived(t, h)
+        for i in range(4):
+            e_place(t, h, pick, i)
 
     def e_second(t, c, h):
         for qo in (2, 1, 3):
@@ -319,11 +332,18 @@
         for h in (0, 1):
             em[t - 1, h, ROWS[c]] = e_final(t, c, h).astype(BF16)
 
-    for h in (0, 1):
-        e_middle(0, h)
-        e_second(0, 0, h)
-    for h in (0, 1):
-        e_second(0, 1, h)
+    picks = [e_pick(0, h) for h in (0, 1)]
+    for half in (0, 1):
+        for h in (0, 1):
+            e1_arrived(0, h, slice(2 * half, 2 * half + 2))
+            for i in (2 * half, 2 * half + 1):
+                e_place(0, h, picks[h], i)
+                if QOFF[i]:
+                    e2(0, 0, h, QOFF[i]).start()
+        for h in (0, 1):
+            for i in (2 * half, 2 * half + 1):
+                if QOFF[i]:
+                    e2(0, 1, h, QOFF[i]).start()
     for po in (2, 1, 3):
         e_first(1, po)
     for c in (0, 1):
@@ -350,10 +370,10 @@
     for t in range(1, STEPS + 1):
         begin(t, 0)
         emission(t, 3)
-        emission(t, 4)
         if t > 1:
             finish(t - 1, 1)
         rs_merge(t, 0)
+        emission(t, 4)
         emission(t, 5)
         if t > 1:
             ag_relay(t - 1, 1, (0, 1, 2))
@@ -362,8 +382,8 @@
         store_emitted(t, 0)
         finish(t, 0)
         emission(t + 1, 0)
+        rs_merge(t, 1)
         emission(t + 1, 1)
-        rs_merge(t, 1)
         emission(t + 1, 2)
         if t < STEPS:
             ag_relay(t, 0, (0, 1, 2))
@@ -453,7 +473,7 @@
             dma,
             dma((32,)),
             dma((STEPS + 1,)),
-            dma((STEPS + 1, 2)),
+            dma((STEPS + 1, 2, 2)),
             dma((2,)),
             dma((STEPS + 1, 2, 2)),
             dma((2, 2)),

time: 132 us -> 130 us (0.985)
  Pallas kernels: 131 us -> 129 us
    pallas_call x1, Pallas kernels: 129 us -> 127 us  [on_device(): pl.pallas_call(kernel, out_shape=(jax.ShapeDtypeStruct((SEQS, 2 * BLOCK),...]
where the time goes in v6:
time: 130 us
  Pallas kernels  129 us (99%)
    pallas_call x1, Pallas kernels, on_device(): pl.pallas_call(kernel, out_shape=(jax.ShapeDtypeStruct((SEQS, 2 * BLOCK),...  127 us

profile of v6, /device:TPU:1, one launch (start us, length us, event | category | flops | bytes accessed | tf_op | source)
XLA Modules:
  0.0 129.7 jit_solution(13572732049309778538)
XLA Ops:
  0.6 127.2 %forward.1 = (f32[104,1024]{1,0:T(8,128)}, f32[8,128]{1,0:T(8,128)}) custom-call(s32[32]{0:T(128)} %bitcast.4, s32[4,104]{1,0:T(4,128)} %tok_ref.1, bf16[32,512,512]{2,1,0:T(8,128)(2,1)} %bitcast.3, bf16[313,16384]{1,0:T(8,128)(2,1)} %emis_hbm.1), custom_call_target="tpu_custom_call" | custom-call | tf_op jit(solution)/shard_map/forward/pallas_call | solution.py:440
  127.9 1.8 %normalize.1 = (bf16[104,1024]{1,0:T(8,128)(2,1)}, f32[1,104]{1,0:T(1,128)}) custom-call(f32[104,1024]{1,0:T(8,128)} %get-tuple-element.6.weights_ref, f32[8,128]{1,0:T(8,128)} %get-tuple-element.7.scale_ref), custom_call_target="tpu_custom_call" | custom-call | tf_op jit(solution)/shard_map/normalize/pallas_call | solution.py:491

commit v7 on v6

--- a/solution.py
+++ b/solution.py
@@ -12,6 +12,7 @@
 SEQS = 104
 CAP = 26
 SLOT = 32
+TIGHT = 80
 BLOCK = 512
 STEPS = 3
 ROWS = (slice(0, 48), slice(48, 104))
@@ -26,7 +27,7 @@
 
 def kernel(
     ids_ref, tok_ref, blocks_hbm, emis_hbm, wfin, scale_ref,
-    blocks_v, emis_v, sel_v, pack, land1, land2_a, land2_b, mid_a, mid_b, own, em, states_a, states_b, states_c, states_d, part_a, part_b, rs_a, rs_b, ar0, ar1, ar2,
+    blocks_v, emis_v, sel_v, pack, pack_c, land1, land1_c, land2_a, land2_b, mid_a, mid_b, own, em, states_a, states_b, states_c, states_d, part_a, part_b, rs_a, rs_b, ar0, ar1, ar2,
     blk_sem, emis_sem, e_send, e_recv, e_send2, e_recv2, ag_send, ag_recv, rs_send, rs_recv, a_send, a_recv,
 ):
     row = lax.axis_index("row")
@@ -35,6 +36,8 @@
     x, z = col // 4, col % 4
     vocab = emis_v.shape[1]
     states = (states_a, states_b, states_c, states_d)
+    packs = [pack.at[t] for t in range(STEPS)] + [pack_c]
+    lands = [land1.at[t] for t in range(STEPS)] + [land1_c]
     land2 = (land2_a, land2_b)
     mid = (mid_a, mid_b)
     part = (part_a, part_b)
@@ -109,22 +112,26 @@
         pos_row = jnp.sum(same, axis=0, keepdims=True)
         return tok_row, owner_row, owner_col, pos_row
 
-    for t in range(STEPS + 1):
-        tok_row, owner_row, owner_col, pos_row = places(t)
-        me = col.astype(F32)
-        slot_of = jnp.where((pos_row == iota((SLOT, SEQS), 0)) & (owner_row == me), 1.0, 0.0).astype(BF16)
+    me = col.astype(F32)
+
+    def chosen(t, rows, start):
+        tok_row, owner_row, _, pos_row = places(t)
+        slot_of = jnp.where((pos_row + float(start) == iota((rows, SEQS), 0)) & (owner_row == me), 1.0, 0.0).astype(BF16)
         id_of = jnp.where(to_col(tok_row) - me * float(vocab) == iota((SEQS, vocab), 1), 1.0, 0.0).astype(BF16)
-        sel_v[t * SLOT : (t + 1) * SLOT, :] = jnp.dot(slot_of, id_of, preferred_element_type=F32).astype(BF16)
+        return jnp.dot(slot_of, id_of, preferred_element_type=F32)
+
+    sel_v[:SLOT, :] = chosen(0, SLOT, 0).astype(BF16)
+    sel_v[SLOT:, :] = sum(chosen(t, TIGHT, CAP * (t - 1)) for t in range(1, STEPS + 1)).astype(BF16)
 
     def e1(t, h, po, part=slice(0, 4)):
         p, _ = pq(h)
         return remote(
-            pack.at[t, h, po - 1, part], land1.at[t, h, part, p], e_send.at[t], e_recv.at[t, h, part.start // 2],
+            packs[t].at[h, po - 1, part], lands[t].at[h, part, p], e_send.at[t], e_recv.at[t, h, part.start // 2],
             along(h, True, po),
         )
 
     def e1_arrived(t, h, part=slice(0, 4)):
-        three = land1.at[t, h, part, 0:3]
+        three = lands[t].at[h, part, 0:3]
         remote(three, three, e_send.at[t], e_recv.at[t, h, part.start // 2], sib).wait_recv()
 
     def e2(t, c, h, qo):
@@ -139,11 +146,11 @@
                 emis_copy(chunk).wait()
                 rows = jnp.dot(sel_v[...], emis_v[chunk], preferred_element_type=F32).astype(BF16)
                 for t in range(STEPS + 1):
-                    piece = rows[t * SLOT : (t + 1) * SLOT]
+                    piece = rows[t * SLOT : min((t + 1) * SLOT, SLOT + TIGHT)]
                     if po:
-                        pack[t, h, po - 1, i] = piece
+                        packs[t][h, po - 1, i] = piece
                     else:
-                        land1[t, h, i, p] = piece
+                        lands[t][h, i, p] = piece
             if (half, po, h) == (0, 2, 0):
                 pl.semaphore_wait(barrier, 22)
             if po:
@@ -165,12 +172,20 @@
             x_of += jnp.where(owner_col >= float(4 * k), 1.0, 0.0)
         z_of = owner_col - 4.0 * x_of
         p_of, q_of = (x_of, z_of) if h == 0 else (z_of, x_of)
-        place = p_of * float(SLOT) + to_col(pos_row)
-        lane = iota((SEQS, 4 * SLOT), 1)
-        return jnp.where((lane == place) & (q_of == q.astype(F32)), 1.0, 0.0).astype(BF16)
-
-    def e_place(t, h, pick, i):
-        rows = jnp.dot(pick, land1[t, h, i].reshape(4 * SLOT, BLOCK), preferred_element_type=F32).astype(BF16)
+        place = to_col(pos_row) + float(CAP * max(t - 1, 0))
+        picks = []
+        for n in ((0,), (1,), (1, 2), (2, 3))[t]:
+            width = lands[n].shape[3]
+            there = place - float(SLOT * max(n - 1, 0))
+            mine = (there >= 0.0) & (there < float(width)) & (q_of == q.astype(F32))
+            lane = iota((SEQS, 4 * width), 1)
+            picks.append((n, jnp.where((lane == p_of * float(width) + there) & mine, 1.0, 0.0).astype(BF16)))
+        return picks
+
+    def e_place(t, h, picks, i):
+        rows = sum(
+            jnp.dot(pick, lands[n][h, i].reshape(-1, BLOCK), preferred_element_type=F32) for n, pick in picks
+        ).astype(BF16)
         if QOFF[i]:
             for c in (0, 1):
                 mid[c][h, QOFF[i] - 1] = rows[ROWS[c]]
@@ -420,7 +435,7 @@
         ag_sent(STEPS - 1, c)
     e_sent2()
     for t in range(STEPS + 1):
-        remote(pack.at[t], pack.at[t], e_send.at[t], e_recv.at[t, 0], sib).wait_send()
+        remote(packs[t], packs[t], e_send.at[t], e_recv.at[t, 0, 0], sib).wait_send()
     seven.wait_send()
     fifteen.wait_send()
 
@@ -450,9 +465,11 @@
         scratch_shapes=[
             vmem((32, BLOCK, BLOCK), BF16),
             vmem((32, vocab, BLOCK), BF16),
-            vmem((4 * SLOT, vocab), BF16),
-            vmem((STEPS + 1, 2, 3, 4, SLOT, BLOCK), BF16),
-            vmem((STEPS + 1, 2, 4, 4, SLOT, BLOCK), BF16),
+            vmem((SLOT + TIGHT, vocab), BF16),
+            vmem((STEPS, 2, 3, 4, SLOT, BLOCK), BF16),
+            vmem((2, 3, 4, TIGHT - 2 * SLOT, BLOCK), BF16),
+            vmem((STEPS, 2, 4, 4, SLOT, BLOCK), BF16),
+            vmem((2, 4, 4, TIGHT - 2 * SLOT, BLOCK), BF16),
             vmem((STEPS + 1, 2, 3, 48, BLOCK), BF16),
             vmem((STEPS + 1, 2, 3, 56, BLOCK), BF16),
             vmem((2, 3, 48, BLOCK), BF16),

time: 130 us -> 126 us (0.969)
  Pallas kernels: 129 us -> 126 us
    pallas_call x1, Pallas kernels: 127 us -> 124 us  [on_device(): pl.pallas_call(kernel, out_shape=(jax.ShapeDtypeStruct((SEQS, 2 * BLOCK),...]
where the time goes in v7:
time: 126 us
  Pallas kernels  126 us (100%)
    pallas_call x1, Pallas kernels, on_device(): pl.pallas_call(kernel, out_shape=(jax.ShapeDtypeStruct((SEQS, 2 * BLOCK),...  124 us

profile of v7, /device:TPU:1, one launch (start us, length us, event | category | flops | bytes accessed | tf_op | source)
XLA Modules:
  0.0 126.3 jit_solution(9399172190868386990)
XLA Ops:
  0.6 123.9 %forward.1 = (f32[104,1024]{1,0:T(8,128)}, f32[8,128]{1,0:T(8,128)}) custom-call(s32[32]{0:T(128)} %bitcast.4, s32[4,104]{1,0:T(4,128)} %tok_ref.1, bf16[32,512,512]{2,1,0:T(8,128)(2,1)} %bitcast.3, bf16[313,16384]{1,0:T(8,128)(2,1)} %emis_hbm.1), custom_call_target="tpu_custom_call" | custom-call | tf_op jit(solution)/shard_map/forward/pallas_call | solution.py:455
  124.5 1.8 %normalize.1 = (bf16[104,1024]{1,0:T(8,128)(2,1)}, f32[1,104]{1,0:T(1,128)}) custom-call(f32[104,1024]{1,0:T(8,128)} %get-tuple-element.6.weights_ref, f32[8,128]{1,0:T(8,128)} %get-tuple-element.7.scale_ref), custom_call_target="tpu_custom_call" | custom-call | tf_op jit(solution)/shard_map/normalize/pallas_call | solution.py:508
